TPU v7x, 128 devices: a whole 4x4x4 slice. The times are simulated.
128 devices in a mesh: dp: 8 (over z, core), seq: 16 (over y, x).
Axes of the slice: x: 4, y: 4, z: 4, core: 2. Of those that a mesh axis runs over, the one named last changes fastest.
Arguments:
- tokens: bfloat16 [8192, 3584], P(('dp', 'seq')), may hold values from -6 to 6
- gain: float32 [3584], replicated, may hold values from 0.25 to 1.75
- q_weight: bfloat16 [3584, 2048], P(('dp', 'seq')), may hold values from -0.09375 to 0.09375
- key_value_weight: bfloat16 [3584, 768], P(('dp', 'seq')), may hold values from -0.09375 to 0.09375
- q_bias: float32 [2048], replicated, may hold values from -8 to 8
- kv_bias: float32 [768], replicated, may hold values from -8 to 8
- plan: int32 [8, 16], replicated, may hold values from 0 to 7, as said below
- home_offsets: int32 [8, 16], replicated, may hold values from 0 to 15, as said below
Outputs:
- attended: bfloat16 [8192, 2048], P(('dp', 'seq'))
- kv_cache: bfloat16 [8, 16, 512, 768], P('dp', 'seq')
Inputs may be any that keep to these rules, and one draw needn't show every extreme that they name: `plan`: all stretches of a home row have one group; no group gets more than two home rows, and some group gets two. `home_offsets`: each home row holds one or two sequences of consecutive stretches; the value is the column where the stretch's sequence begins.
All inputs are finite; a program needn't handle non-finite values.
Results may differ from a plain program's by a relative error of at most 0.0096.
Values may be sent and summed in bfloat16 or wider, within the bound.
No kernel may reach another device: no remote copies, remote signals or barrier semaphores. Data moves between devices by JAX's collectives and lax.ppermute only.
A program may use at most 128 MiB of HBM per device.

v0:
```python
import functools

import jax
import jax.numpy as jnp
import numpy as np
from jax import lax
from jax.experimental import pallas as pl
from jax.experimental.pallas import tpu as pltpu
from jax.sharding import Mesh
from jax.sharding import PartitionSpec as P

HEAD = 128
NEG = -1e30
ROW_TOK = 256
COLS = 768

EVERY = ("z", "core", "y", "x")
SIZES = (4, 2, 4, 4)
VM = pl.BlockSpec(memory_space=pltpu.VMEM)
SM = pl.BlockSpec(memory_space=pltpu.SMEM)
ANY = pl.BlockSpec(memory_space=pl.ANY)


def rotary_table():
    angles = np.arange(1024)[:, None] * 1000000.0 ** (-np.arange(64) * 2.0 / HEAD)[None, :]
    return np.concatenate([np.cos(angles), np.sin(angles)], axis=1).astype(np.float32)


def flat(z, c, y, x):
    return ((z % 4 * 2 + c % 2) * 4 + y % 4) * 4 + x % 4


PLACES = [(z, c, y, x) for z in range(4) for c in range(2) for y in range(4) for x in range(4)]


def send(v, move):
    return lax.ppermute(v, EVERY, [(flat(*p), flat(*move(*p))) for p in PLACES])


def spread(one):
    return [one(j) for j in (2, 1, 3)]


HOPS = (0, 2, 1, 3)


def along_x(j):
    return lambda z, c, y, x: (z, c, y, x + j)


def along_z(j):
    return lambda z, c, y, x: (z + j, c, y, x)


def along_first(j):
    return lambda z, c, y, x: (z + j, c, y, x) if c == 0 else (z, c, y + j, x)


def along_second(j):
    return lambda z, c, y, x: (z, c, y + j, x) if c == 0 else (z + j, c, y, x)


def other_core(z, c, y, x):
    return (z, 1 - c, y, x)


def along_y(j):
    return lambda z, c, y, x: (z, c, y + j, x)


def pair_x(z, c, y, x):
    return (z, c, y, x ^ 1)


def call(kernel, outs, operands, in_specs=None, scratch=(), grant=20, **more):
    outs = tuple(jax.ShapeDtypeStruct(s, d) for s, d in outs)
    return pl.pallas_call(
        kernel,
        out_shape=outs,
        in_specs=[VM] * len(operands) if in_specs is None else in_specs,
        out_specs=(VM,) * len(outs),
        scratch_shapes=list(scratch),
        compiler_params=pltpu.CompilerParams(vmem_limit_bytes=grant * 1024 * 1024),
        name=kernel.__name__,
        **more,
    )(*operands)


def cut(wq, wkv, b0, b1, b2, b3, q_buf, kv_buf, sem):
    copies = [
        pltpu.make_async_copy(wq, q_buf, sem.at[0]),
        pltpu.make_async_copy(wkv, kv_buf, sem.at[1]),
    ]
    for copy in copies:
        copy.start()
    for copy in copies:
        copy.wait()
    x = lax.axis_index("x")
    for j, block in enumerate((b0, b1, b2, b3)):
        to = lax.rem(x + j, 4)
        slot = lax.div(to + 1, 2)
        for n in range(2):
            low = pl.multiple_of((slot + 3 * n) * HEAD, HEAD)
            block[:, n * HEAD : (n + 1) * HEAD] = kv_buf[:, pl.ds(low, HEAD)]
        block[:, 256:] = q_buf[:, pl.ds(pl.multiple_of(to * 512, 512), 512)]


def norm(tokens, gain, after, out):
    floats = tokens[...].astype(jnp.float32)
    mean = jnp.mean(floats * floats, axis=1, keepdims=True)
    out[...] = (floats * lax.rsqrt(mean + 1e-06) * gain[...][None, :]).astype(jnp.bfloat16)


def keep(v, out, sem):
    copy = pltpu.make_async_copy(v, out, sem)
    copy.start()
    copy.wait()


def place(p0, p2, p1, p3, out, buf):
    x = lax.axis_index("x")
    for j, p in zip(HOPS, (p0, p2, p1, p3)):
        buf[lax.rem(x + 4 - j, 4)] = p[...].astype(jnp.float32)
    out[...] = jnp.concatenate([buf[k] for k in range(4)], axis=0).astype(jnp.bfloat16)


def stage(s0, s2, s1, s3, after, block):
    for i, s in enumerate((s0, s1, s2, s3)):
        block[i] = s[...]


def relay(n1, n3, s0, s1, s3, joined, r1, r3, low, high):
    for n, s in enumerate((s0, s1, s3)):
        joined[4 * n : 4 * n + 4] = s[...]
    r1[...] = s1[:2]
    r3[...] = s3[2:]
    low[...] = n1[:32, :]
    high[...] = n3[32:, :]


def join2(after1, after2, a, b, out):
    out[:2] = a[...]
    out[2:] = b[...]


def load_weights(ref, t, places, buf):
    y = lax.axis_index("y")
    z = lax.axis_index("z")
    for n, (j, i) in enumerate(places):
        zz = lax.rem(z + jnp.where(t == 0, i, j), 4)
        yy = lax.rem(y + jnp.where(t == 0, j, i), 4)
        buf[(2 * zz + t) * 4 + yy] = ref[n]


FIRST = [(j, i) for j in (0, 1, 3) for i in range(4)]
LAST = [(2, i) for i in range(4)]


def gather(
    offsets, own1, own2, other1, n0, n1, n2a, n2b, n3, table, qb, kvb, w, x_out, cs, qb_out, kvb_out, sem
):
    e = 2 * lax.axis_index("z") + lax.axis_index("core")
    y = lax.axis_index("y")
    x = lax.axis_index("x")
    core = lax.axis_index("core")
    copies = []
    for k in range(4):
        s = 4 * y + k
        row = pl.multiple_of((s - offsets[e, s]) * 64, 64)
        copies.append(
            pltpu.make_async_copy(
                table.at[pl.ds(row, 64), :], cs.at[k * 64 : (k + 1) * 64, :], sem.at[k]
            )
        )
    copies.append(
        pltpu.make_async_copy(qb.at[pl.ds(pl.multiple_of(x * 512, 512), 512)], qb_out, sem.at[4])
    )
    slot = lax.div(x + 1, 2)
    for n in range(2):
        low = pl.multiple_of((slot + 3 * n) * HEAD, HEAD)
        copies.append(
            pltpu.make_async_copy(kvb.at[pl.ds(low, HEAD)], kvb_out.at[n], sem.at[5 + n])
        )
    for copy in copies:
        copy.start()
    for ref, j, low, size in (
        (n0, 0, 0, 64),
        (n1, 1, 0, 64),
        (n2a, 2, 0, 32),
        (n2b, 2, 32, 32),
        (n3, 3, 0, 64),
    ):
        row = pl.multiple_of(lax.rem(x + j, 4) * 64 + low, 32)
        x_out[pl.ds(row, size), :] = ref[...]
    load_weights(own1, core, FIRST, w)
    load_weights(own2, core, LAST, w)
    load_weights(other1, 1 - core, FIRST, w)
    for copy in copies:
        copy.wait()


def rotate(v, cos, sin):
    a = v[:, :64]
    b = v[:, 64:]
    return jnp.concatenate([a * cos - b * sin, b * cos + a * sin], axis=1).astype(jnp.bfloat16)


def kv_project(w_in, other2, x_in, cs, kvb, w, kv):
    del w_in
    load_weights(other2, 1 - lax.axis_index("core"), LAST, w)
    acc = jnp.dot(
        x_in[...], w[:, :, :256].reshape(3584, 256), preferred_element_type=jnp.float32
    )
    kv[:, :HEAD] = rotate(acc[:, :HEAD] + kvb[0][None, :], cs[:, :64], cs[:, 64:])
    kv[:, HEAD:] = (acc[:, HEAD:] + kvb[1][None, :]).astype(jnp.bfloat16)


def q_project(w, x_in, cs, qb, q):
    for g in range(2):
        part = slice((g + 1) * 256, (g + 2) * 256)
        acc = jnp.dot(
            x_in[...], w[:, :, part].reshape(3584, 256), preferred_element_type=jnp.float32
        )
        for h in range(2):
            low = (2 * g + h) * HEAD
            head = acc[:, h * HEAD : (h + 1) * HEAD] + qb[low : low + HEAD][None, :]
            q[:, low : low + HEAD] = rotate(head, cs[:, :64], cs[:, 64:])


def one_head(qh, blocks, mask):
    parts = []
    for j, kv in enumerate(blocks):
        s = lax.dot_general(
            qh, kv[:, :HEAD], (((1,), (1,)), ((), ())), preferred_element_type=jnp.float32
        )
        parts.append(s * (HEAD**-0.5) + mask[:, j * ROW_TOK : (j + 1) * ROW_TOK])
    top = functools.reduce(jnp.maximum, [jnp.max(s, axis=1, keepdims=True) for s in parts])
    mass = jnp.zeros((ROW_TOK, 1), jnp.float32)
    acc = jnp.zeros((ROW_TOK, HEAD), jnp.float32)
    for s, kv in zip(parts, blocks):
        p = jnp.exp(s - top)
        mass += jnp.sum(p, axis=1, keepdims=True)
        acc += jnp.dot(p.astype(jnp.bfloat16), kv[:, HEAD:], preferred_element_type=jnp.float32)
    return (acc / mass).astype(jnp.bfloat16)


def attend_own(offsets, q, a0, a1, a2, a3, after, mask, last):
    y = lax.axis_index("y")
    e = 2 * lax.axis_index("z") + lax.axis_index("core")
    qi = lax.broadcasted_iota(jnp.int32, (ROW_TOK, ROW_TOK), 0)
    ki = lax.broadcasted_iota(jnp.int32, (ROW_TOK, ROW_TOK), 1)
    starts = [offsets[e, 4 * y + k] * 64 for k in range(4)]
    start = jnp.where(
        qi < 128,
        jnp.where(qi < 64, starts[0], starts[1]),
        jnp.where(qi < 192, starts[2], starts[3]),
    )
    for j in range(4):
        key = ki + lax.rem(y + j, 4) * ROW_TOK
        ok = (key >= start) & (key <= qi + y * ROW_TOK)
        mask[:, j * ROW_TOK : (j + 1) * ROW_TOK] = jnp.where(ok, 0.0, NEG)
    last[...] = one_head(q[:, 3 * HEAD :], [a[...] for a in (a0, a1, a2, a3)], mask)


def attend(mask, last, q, a0, a1, a2, a3, b0, b1, b2, b3, o0, o1, o2, o3, full):
    x = lax.axis_index("x")
    for h in range(3):
        left = (x == 1) if h == 2 else ((x == 1) | (x == 3))
        pick = jnp.where(left, 1, 0)
        blocks = [
            jnp.where(pick == 1, b[...], a[...])
            for a, b in ((a0, b0), (a1, b1), (a2, b2), (a3, b3))
        ]
        part = slice(h * HEAD, (h + 1) * HEAD)
        full[:, part] = one_head(q[:, part], blocks, mask)
    full[:, 3 * HEAD :] = last[...]
    for j, o in enumerate((o0, o1, o2, o3)):
        o[...] = full[pl.ds(pl.multiple_of(lax.rem(x + j, 4) * 64, 64), 64), :]


def cache_rows(a0, a2, a1, a3, after1, after2, t0, t1, t2, t3):
    x = lax.axis_index("x")
    y = lax.axis_index("y")
    i = lax.broadcasted_iota(jnp.int32, (64, ROW_TOK), 0)
    t = lax.broadcasted_iota(jnp.int32, (64, ROW_TOK), 1)
    want = 16 * lax.rem(i, 16) + 4 * y + lax.rem(x + lax.div(i, 16), 4)
    select = jnp.where(t == want, 1.0, 0.0).astype(jnp.bfloat16)
    for j, a in zip(HOPS, (a0, a2, a1, a3)):
        got = jnp.dot(select, a[...], preferred_element_type=jnp.float32).astype(jnp.bfloat16)
        rows = pl.ds(pl.multiple_of(lax.rem(y + j, 4) * 16, 16), 16)
        for k, out in enumerate((t0, t1, t2, t3)):
            out[rows, :] = got[16 * k : 16 * k + 16]


def cache_heads(t0, t2, t1, t3, out, buf):
    x = lax.axis_index("x")
    for j, t in zip(HOPS, (t0, t2, t1, t3)):
        buf[lax.rem(x + 4 - j, 4)] = t[...]
    for k, src in enumerate((0, 1, 3)):
        out[:, k * HEAD : (k + 1) * HEAD] = buf[src, :, :HEAD]
        out[:, (3 + k) * HEAD : (4 + k) * HEAD] = buf[src, :, HEAD:]


def cache_join(c0, c2, c1, c3, after, out):
    for n, c in zip(HOPS, (c0, c2, c1, c3)):
        out[n] = c[...]


def finish(plan, own, other, r0, r2, r1, r3, attended, cache):
    x = lax.axis_index("x")
    for j, r in zip(HOPS, (r0, r2, r1, r3)):
        low = pl.multiple_of(lax.rem(x + 4 - j, 4) * 512, 512)
        attended[:, pl.ds(low, 512)] = r[...]
    z = lax.axis_index("z")
    core = lax.axis_index("core")
    group = 2 * z + core
    for ref, t in ((own, core), (other, 1 - core)):
        for j in range(4):
            e = 2 * lax.rem(z + j, 4) + t
            rows = pl.ds(pl.multiple_of(e * 64, 64), 64)
            v = ref[j]
            cache[0, 0, rows, :] = jnp.where(plan[e, 0] == group, v, jnp.zeros_like(v))


def per_device(tokens, gain, q_weight, key_value_weight, q_bias, kv_bias, plan, home_offsets):
    bf = jnp.bfloat16
    f32 = jnp.float32
    blocks = call(
        cut,
        [((28, COLS), bf)] * 4,
        (q_weight, key_value_weight),
        [ANY] * 2,
        [
            pltpu.VMEM((28, 2048), bf),
            pltpu.VMEM((28, 768), bf),
            pltpu.SemaphoreType.DMA((2,)),
        ],
        grant=60,
    )
    (kept,) = call(keep, [((28, COLS), bf)], (blocks[0],), [ANY], [pltpu.SemaphoreType.DMA])
    got = [kept] + spread(lambda j: send(blocks[j], along_x(j)))
    (w0,) = call(place, [((112, COLS), bf)], got, scratch=[pltpu.VMEM((4, 28, COLS), f32)])
    (n0,) = call(norm, [((64, 3584), bf)], (tokens, gain, w0), [VM, VM, ANY])
    (s0,) = call(
        stage,
        [((4, 112, COLS), bf)],
        (w0, *spread(lambda j: send(w0, along_first(-j))), n0),
        [VM] * 4 + [ANY],
    )
    n1 = send(n0, along_x(-1))
    n3 = send(n0, along_x(1))
    s1 = send(s0, along_second(-1))
    s3 = send(s0, along_second(1))
    own1, r1, r3, low, high = call(
        relay,
        [((12, 112, COLS), bf)] + [((2, 112, COLS), bf)] * 2 + [((32, 3584), bf)] * 2,
        (n1, n3, s0, s1, s3),
    )
    n2a = send(low, along_x(-1))
    n2b = send(high, along_x(1))
    s2a = send(r1, along_second(-1))
    s2b = send(r3, along_second(1))
    other1 = send(own1, other_core)
    (own2,) = call(
        join2, [((4, 112, COLS), bf)], (n2a, n2b, s2a, s2b), [ANY] * 2 + [VM] * 2
    )
    other2 = send(own2, other_core)
    w, x_all, cs, qb, kvb = call(
        gather,
        [
            ((32, 112, COLS), bf),
            ((ROW_TOK, 3584), bf),
            ((ROW_TOK, HEAD), f32),
            ((512,), f32),
            ((2, HEAD), f32),
        ],
        (
            home_offsets, own1, own2, other1, n0, n1, n2a, n2b, n3,
            jnp.asarray(rotary_table()), q_bias, kv_bias,
        ),
        [SM] + [VM] * 8 + [ANY] * 3,
        [pltpu.SemaphoreType.DMA((7,))],
    )
    w, kv = call(
        kv_project,
        [((32, 112, COLS), bf), ((ROW_TOK, 256), bf)],
        (w, other2, x_all, cs, kvb),
        input_output_aliases={0: 0},
    )
    (q,) = call(q_project, [((ROW_TOK, 512), bf)], (w, x_all, cs, qb))

    a2, a1, a3 = spread(lambda j: send(kv, along_y(-j)))
    a = [kv, a1, a2, a3]
    b = [send(v, pair_x) for v in a]
    rows = call(cache_rows, [((64, 256), bf)] * 4, (kv, a2, a1, a3, q, b[0]), [VM] * 4 + [ANY] * 2)
    (mine,) = call(
        cache_heads,
        [((64, 768), bf)],
        (rows[0], *spread(lambda j: send(rows[j], along_x(j)))),
        scratch=[pltpu.VMEM((4, 64, 256), bf)],
    )
    mask, last = call(
        attend_own,
        [((ROW_TOK, 1024), f32), ((ROW_TOK, HEAD), bf)],
        (home_offsets, q, *a, mine),
        [SM] + [VM] * 5 + [ANY],
    )
    outs = call(
        attend,
        [((64, 512), bf)] * 4,
        (mask, last, q, *a, *b),
        scratch=[pltpu.VMEM((ROW_TOK, 512), bf)],
    )
    (cached,) = call(
        cache_join,
        [((4, 64, 768), bf)],
        (mine, *spread(lambda j: send(mine, along_z(-j))), outs[0]),
        [VM] * 4 + [ANY],
    )
    attended, cache = call(
        finish,
        [((64, 2048), bf), ((1, 1, 512, 768), bf)],
        (
            plan,
            cached,
            send(cached, other_core),
            outs[0],
            *spread(lambda j: send(outs[j], along_x(j))),
        ),
        [SM] + [VM] * 6,
    )
    return attended, cache


def solution(mesh):
    fine = Mesh(mesh.devices.reshape(SIZES), EVERY)
    in_specs = (P(EVERY, None), P(), P(EVERY, None), P(EVERY, None), P(), P(), P(), P())
    out_specs = (P(EVERY, None), P(("z", "core"), ("y", "x"), None, None))
    return jax.shard_map(
        per_device, mesh=fine, in_specs=in_specs, out_specs=out_specs, check_vma=False
    )
```

profile of v0, /device:TPU:6, one launch (start us, length us, event | category | flops | bytes accessed | tf_op | source)
XLA Modules:
  0.0 91.5 jit_solution(5334363856443296041)
XLA Ops:
  0.6 1.6 %cut.1 = (bf16[28,768]{1,0:T(8,128)(2,1)}, bf16[28,768]{1,0:T(8,128)(2,1)}, bf16[28,768]{1,0:T(8,128)(2,1)}, bf16[28,768]{1,0:T(8,128)(2,1)}) custom-call(bf16[28,2048]{1,0:T(8,128)(2,1)} %wq.1, bf16[28,768]{1,0:T(8,128)(2,1)} %wkv.1), custom_call_target="tpu_custom_call" | custom-call | tf_op jit(solution)/shard_map/cut/pallas_call | solution.py:77
  2.2 1.5 %collective-permute-start = (bf16[28,768]{1,0:T(8,128)(2,1)}, bf16[28,768]{1,0:T(8,128)(2,1)S(1)}, u32[]{:S(2)}, u32[]{:S(2)}) collective-permute-start(bf16[28,768]{1,0:T(8,128)(2,1)} %get-tuple-element.29), channel_id=1, source_target_pairs={{0,2},{1,3},{2,0},{3,1},{4,6},{5,7},{6,4},{7,5},{8,10},{9,11},{10,... | collective-permute-start | bytes 129032 | tf_op jit(solution)/shard_map/ppermute | solution.py:37
  3.7 2.1 %collective-permute-start.1 = (bf16[28,768]{1,0:T(8,128)(2,1)}, bf16[28,768]{1,0:T(8,128)(2,1)S(1)}, u32[]{:S(2)}, u32[]{:S(2)}) collective-permute-start(bf16[28,768]{1,0:T(8,128)(2,1)} %get-tuple-element.30), channel_id=1, source_target_pairs={{0,1},{1,2},{2,3},{3,0},{4,5},{5,6},{6,7},{7,4},{8,9},{9,10},{10,1... | collective-permute-start | bytes 129032 | tf_op jit(solution)/shard_map/ppermute | solution.py:37
  6.7 1.6 %collective-permute-done.p2 = bf16[28,768]{1,0:T(8,128)(2,1)S(1)} collective-permute-done((bf16[28,768]{1,0:T(8,128)(2,1)}, bf16[28,768]{1,0:T(8,128)(2,1)S(1)}, u32[]{:S(2)}, u32[]{:S(2)}) %collective-permute-start) | collective-permute-done | bytes 43040 | tf_op jit(solution)/shard_map/ppermute | solution.py:37
  8.3 3.0 %collective-permute-done.2.p3 = bf16[28,768]{1,0:T(8,128)(2,1)S(1)} collective-permute-done((bf16[28,768]{1,0:T(8,128)(2,1)}, bf16[28,768]{1,0:T(8,128)(2,1)S(1)}, u32[]{:S(2)}, u32[]{:S(2)}) %collective-permute-start.2) | collective-permute-done | bytes 43040 | tf_op jit(solution)/shard_map/ppermute | solution.py:37
  11.4 4.0 %collective-permute-start.5 = (bf16[112,768]{1,0:T(8,128)(2,1)S(1)}, bf16[112,768]{1,0:T(8,128)(2,1)S(1)}, u32[]{:S(2)}, u32[]{:S(2)}) collective-permute-start(bf16[112,768]{1,0:T(8,128)(2,1)S(1)} %place.1.after.s0), channel_id=1, source_target_pairs={{0,64},{1,65},{2,66},{3,67},{4,68},{5,69},{6,70},{7,71},{8,72},{9,... | collective-permute-start | bytes 516104 | tf_op jit(solution)/shard_map/ppermute | solution.py:37
  16.1 1.3 %collective-permute-start.7 = (bf16[112,768]{1,0:T(8,128)(2,1)S(1)}, bf16[112,768]{1,0:T(8,128)(2,1)S(1)}, u32[]{:S(2)}, u32[]{:S(2)}) collective-permute-start(bf16[112,768]{1,0:T(8,128)(2,1)S(1)} %place.1.after.s0), channel_id=1, source_target_pairs={{0,32},{1,33},{2,34},{3,35},{4,36},{5,37},{6,38},{7,39},{8,40},{9,... | collective-permute-start | bytes 516104 | tf_op jit(solution)/shard_map/ppermute | solution.py:37
  19.3 2.3 %collective-permute-done.6.s1 = bf16[112,768]{1,0:T(8,128)(2,1)S(1)} collective-permute-done((bf16[112,768]{1,0:T(8,128)(2,1)S(1)}, bf16[112,768]{1,0:T(8,128)(2,1)S(1)}, u32[]{:S(2)}, u32[]{:S(2)}) %collective-permute-start.6) | collective-permute-done | bytes 172064 | tf_op jit(solution)/shard_map/ppermute | solution.py:37
  22.8 3.3 %collective-permute-start.8 = (bf16[4,112,768]{2,1,0:T(8,128)(2,1)S(1)}, bf16[4,112,768]{2,1,0:T(8,128)(2,1)S(1)}, u32[]{:S(2)}, u32[]{:S(2)}) collective-permute-start(bf16[4,112,768]{2,1,0:T(8,128)(2,1)S(1)} %stage.1.s0), channel_id=1, source_target_pairs={{0,12},{1,13},{2,14},{3,15},{4,0},{5,1},{6,2},{7,3},{8,4},{9,5},{1... | collective-permute-start | bytes 2064392 | tf_op jit(solution)/shard_map/ppermute | solution.py:37
  26.1 3.2 %collective-permute-start.4 = (bf16[64,3584]{1,0:T(8,128)(2,1)S(1)}, bf16[64,3584]{1,0:T(8,128)(2,1)S(1)}, u32[]{:S(2)}, u32[]{:S(2)}) collective-permute-start(bf16[64,3584]{1,0:T(8,128)(2,1)S(1)} %norm.1.after.n0), channel_id=1, source_target_pairs={{0,1},{1,2},{2,3},{3,0},{4,5},{5,6},{6,7},{7,4},{8,9},{9,10},{10,1... | collective-permute-start | bytes 1376264 | tf_op jit(solution)/shard_map/ppermute | solution.py:37
  29.3 7.3 %collective-permute-done.3.n1 = bf16[64,3584]{1,0:T(8,128)(2,1)S(1)} collective-permute-done((bf16[64,3584]{1,0:T(8,128)(2,1)S(1)}, bf16[64,3584]{1,0:T(8,128)(2,1)S(1)}, u32[]{:S(2)}, u32[]{:S(2)}) %collective-permute-start.3) | collective-permute-done | bytes 458784 | tf_op jit(solution)/shard_map/ppermute | solution.py:37
  36.6 1.6 %collective-permute-done.9.s3 = bf16[4,112,768]{2,1,0:T(8,128)(2,1)S(1)} collective-permute-done((bf16[4,112,768]{2,1,0:T(8,128)(2,1)S(1)}, bf16[4,112,768]{2,1,0:T(8,128)(2,1)S(1)}, u32[]{:S(2)}, u32[]{:S(2)}) %collective-permute-start.9) | collective-permute-done | bytes 688160 | tf_op jit(solution)/shard_map/ppermute | solution.py:37
  39.4 1.2 %collective-permute-start.13 = (bf16[2,112,768]{2,1,0:T(8,128)(2,1)S(1)}, bf16[2,112,768]{2,1,0:T(8,128)(2,1)S(1)}, u32[]{:S(2)}, u32[]{:S(2)}) collective-permute-start(bf16[2,112,768]{2,1,0:T(8,128)(2,1)S(1)} %get-tuple-element.36), channel_id=1, source_target_pairs={{0,4},{1,5},{2,6},{3,7},{4,8},{5,9},{6,10},{7,11},{8,12},{9,13},{1... | collective-permute-start | bytes 1032200 | tf_op jit(solution)/shard_map/ppermute | solution.py:37
  40.6 3.2 %collective-permute-start.11 = (bf16[32,3584]{1,0:T(8,128)(2,1)S(1)}, bf16[32,3584]{1,0:T(8,128)(2,1)S(1)}, u32[]{:S(2)}, u32[]{:S(2)}) collective-permute-start(bf16[32,3584]{1,0:T(8,128)(2,1)S(1)} %get-tuple-element.34), channel_id=1, source_target_pairs={{0,1},{1,2},{2,3},{3,0},{4,5},{5,6},{6,7},{7,4},{8,9},{9,10},{10,1... | collective-permute-start | bytes 688136 | tf_op jit(solution)/shard_map/ppermute | solution.py:37
  43.8 5.3 %collective-permute-done.10.after1.n2a = bf16[32,3584]{1,0:T(8,128)(2,1)S(1)} collective-permute-done((bf16[32,3584]{1,0:T(8,128)(2,1)S(1)}, bf16[32,3584]{1,0:T(8,128)(2,1)S(1)}, u32[]{:S(2)}, u32[]{:S(2)}) %collective-permute-start.10) | collective-permute-done | bytes 229408 | tf_op jit(solution)/shard_map/ppermute | solution.py:37
  49.4 1.4 %gather.1 = (bf16[32,112,768]{2,1,0:T(8,128)(2,1)S(1)}, bf16[256,3584]{1,0:T(8,128)(2,1)S(1)}, f32[256,128]{1,0:T(8,128)S(1)}, f32[512]{0:T(512)S(1)}, f32[2,128]{1,0:T(2,128)S(1)}) custom-call(s32[8,16]{1,0:T(8,128)S(1)} %copy-done.3, bf16[12,112,768]{2,1,0:T(8,128)(2,1)S(1)} %get-tuple-element.32.own1, bf16[4,112,768]{2,1,0:T(8,128)(2,1)S(1)} %join2.1.own2, ...), custom_call_target="tpu_custom_call" | custom-call | tf_op jit(solution)/shard_map/gather/pallas_call | solution.py:77
  56.2 2.5 %collective-permute-done.17.a1 = bf16[256,256]{1,0:T(8,128)(2,1)S(1)} collective-permute-done((bf16[256,256]{1,0:T(8,128)(2,1)S(1)}, bf16[256,256]{1,0:T(8,128)(2,1)S(1)}, u32[]{:S(2)}, u32[]{:S(2)}) %collective-permute-start.17) | collective-permute-done | bytes 131104 | tf_op jit(solution)/shard_map/ppermute | solution.py:37
  59.5 1.4 %q_project.1.after1.q = bf16[256,512]{1,0:T(8,128)(2,1)S(1)} custom-call(bf16[32,112,768]{2,1,0:T(8,128)(2,1)S(1)} %get-tuple-element.42.w, bf16[256,3584]{1,0:T(8,128)(2,1)S(1)} %get-tuple-element.38.x_in, f32[256,128]{1,0:T(8,128)S(1)} %get-tuple-element.39.cs, f32[512]{0:T(512)S(1)} %get-tuple-element.43.qb), custom_call_target="tpu_custom_call" | custom-call | tf_op jit(solution)/shard_map/q_project/pallas_call | solution.py:77
  61.3 1.7 %collective-permute-done.18.a3 = bf16[256,256]{1,0:T(8,128)(2,1)S(1)} collective-permute-done((bf16[256,256]{1,0:T(8,128)(2,1)S(1)}, bf16[256,256]{1,0:T(8,128)(2,1)S(1)}, u32[]{:S(2)}, u32[]{:S(2)}) %collective-permute-start.18) | collective-permute-done | bytes 131104 | tf_op jit(solution)/shard_map/ppermute | solution.py:37
  63.2 3.1 %collective-permute-start.20 = (bf16[64,256]{1,0:T(8,128)(2,1)S(1)}, bf16[64,256]{1,0:T(8,128)(2,1)S(1)}, u32[]{:S(2)}, u32[]{:S(2)}) collective-permute-start(bf16[64,256]{1,0:T(8,128)(2,1)S(1)} %get-tuple-element.45), channel_id=1, source_target_pairs={{0,2},{1,3},{2,0},{3,1},{4,6},{5,7},{6,4},{7,5},{8,10},{9,11},{10,... | collective-permute-start | bytes 98312 | tf_op jit(solution)/shard_map/ppermute | solution.py:37
  67.1 1.3 %collective-permute-start.22 = (bf16[64,256]{1,0:T(8,128)(2,1)S(1)}, bf16[64,256]{1,0:T(8,128)(2,1)S(1)}, u32[]{:S(2)}, u32[]{:S(2)}) collective-permute-start(bf16[64,256]{1,0:T(8,128)(2,1)S(1)} %get-tuple-element.47), channel_id=1, source_target_pairs={{0,3},{1,0},{2,1},{3,2},{4,7},{5,4},{6,5},{7,6},{8,11},{9,8},{10,9... | collective-permute-start | bytes 98312 | tf_op jit(solution)/shard_map/ppermute | solution.py:37
  70.4 1.8 %collective-permute-done.22.t3 = bf16[64,256]{1,0:T(8,128)(2,1)S(1)} collective-permute-done((bf16[64,256]{1,0:T(8,128)(2,1)S(1)}, bf16[64,256]{1,0:T(8,128)(2,1)S(1)}, u32[]{:S(2)}, u32[]{:S(2)}) %collective-permute-start.22) | collective-permute-done | bytes 32800 | tf_op jit(solution)/shard_map/ppermute | solution.py:37
  72.3 1.6 %collective-permute-start.23 = (bf16[64,768]{1,0:T(8,128)(2,1)S(1)}, bf16[64,768]{1,0:T(8,128)(2,1)S(1)}, u32[]{:S(2)}, u32[]{:S(2)}) collective-permute-start(bf16[64,768]{1,0:T(8,128)(2,1)S(1)} %cache_heads.1.after.c0), channel_id=1, source_target_pairs={{0,64},{1,65},{2,66},{3,67},{4,68},{5,69},{6,70},{7,71},{8,72},{9,... | collective-permute-start | bytes 294920 | tf_op jit(solution)/shard_map/ppermute | solution.py:37
  73.8 1.5 %collective-permute-start.24 = (bf16[64,768]{1,0:T(8,128)(2,1)S(1)}, bf16[64,768]{1,0:T(8,128)(2,1)S(1)}, u32[]{:S(2)}, u32[]{:S(2)}) collective-permute-start(bf16[64,768]{1,0:T(8,128)(2,1)S(1)} %cache_heads.1.after.c0), channel_id=1, source_target_pairs={{0,96},{1,97},{2,98},{3,99},{4,100},{5,101},{6,102},{7,103},{8,104... | collective-permute-start | bytes 294920 | tf_op jit(solution)/shard_map/ppermute | solution.py:37
  76.1 1.2 %attend_own.1 = (f32[256,1024]{1,0:T(8,128)S(1)}, bf16[256,128]{1,0:T(8,128)(2,1)S(1)}) custom-call(s32[8,16]{1,0:T(8,128)S(1)} %copy-done.3, bf16[256,512]{1,0:T(8,128)(2,1)S(1)} %q_project.1.after1.q, bf16[256,256]{1,0:T(8,128)(2,1)S(1)} %get-tuple-element.41.a0, bf16[256,256]{1,0:T(8,128)(2,1)S(1)} %collective-permute-done.17.a1, ...), custom_call_target="tpu_custom_call" | custom-call | tf_op jit(solution)/shard_map/attend_own/pallas_call | solution.py:77
  77.4 1.7 %attend.1 = (bf16[64,512]{1,0:T(8,128)(2,1)S(1)}, bf16[64,512]{1,0:T(8,128)(2,1)S(1)}, bf16[64,512]{1,0:T(8,128)(2,1)S(1)}, bf16[64,512]{1,0:T(8,128)(2,1)S(1)}) custom-call(f32[256,1024]{1,0:T(8,128)S(1)} %get-tuple-element.48.mask, bf16[256,128]{1,0:T(8,128)(2,1)S(1)} %get-tuple-element.49.last, bf16[256,512]{1,0:T(8,128)(2,1)S(1)} %q_project.1.after1.q, ...), custom_call_target="tpu_custom_call" | custom-call | tf_op jit(solution)/shard_map/attend/pallas_call | solution.py:77
  79.8 1.4 %collective-permute-done.25.c3 = bf16[64,768]{1,0:T(8,128)(2,1)S(1)} collective-permute-done((bf16[64,768]{1,0:T(8,128)(2,1)S(1)}, bf16[64,768]{1,0:T(8,128)(2,1)S(1)}, u32[]{:S(2)}, u32[]{:S(2)}) %collective-permute-start.25) | collective-permute-done | bytes 98336 | tf_op jit(solution)/shard_map/ppermute | solution.py:37
  81.3 1.3 %collective-permute-start.30 = (bf16[64,512]{1,0:T(8,128)(2,1)S(1)}, bf16[64,512]{1,0:T(8,128)(2,1)S(1)}, u32[]{:S(2)}, u32[]{:S(2)}) collective-permute-start(bf16[64,512]{1,0:T(8,128)(2,1)S(1)} %get-tuple-element.51), channel_id=1, source_target_pairs={{0,2},{1,3},{2,0},{3,1},{4,6},{5,7},{6,4},{7,5},{8,10},{9,11},{10,... | collective-permute-start | bytes 196616 | tf_op jit(solution)/shard_map/ppermute | solution.py:37
  82.6 1.8 %collective-permute-start.31 = (bf16[64,512]{1,0:T(8,128)(2,1)S(1)}, bf16[64,512]{1,0:T(8,128)(2,1)S(1)}, u32[]{:S(2)}, u32[]{:S(2)}) collective-permute-start(bf16[64,512]{1,0:T(8,128)(2,1)S(1)} %get-tuple-element.52), channel_id=1, source_target_pairs={{0,1},{1,2},{2,3},{3,0},{4,5},{5,6},{6,7},{7,4},{8,9},{9,10},{10,1... | collective-permute-start | bytes 196616 | tf_op jit(solution)/shard_map/ppermute | solution.py:37
  84.6 2.7 %collective-permute-done.30.r2 = bf16[64,512]{1,0:T(8,128)(2,1)S(1)} collective-permute-done((bf16[64,512]{1,0:T(8,128)(2,1)S(1)}, bf16[64,512]{1,0:T(8,128)(2,1)S(1)}, u32[]{:S(2)}, u32[]{:S(2)}) %collective-permute-start.30) | collective-permute-done | bytes 65568 | tf_op jit(solution)/shard_map/ppermute | solution.py:37
  87.3 2.5 %collective-permute-done.32.r3 = bf16[64,512]{1,0:T(8,128)(2,1)S(1)} collective-permute-done((bf16[64,512]{1,0:T(8,128)(2,1)S(1)}, bf16[64,512]{1,0:T(8,128)(2,1)S(1)}, u32[]{:S(2)}, u32[]{:S(2)}) %collective-permute-start.32) | collective-permute-done | bytes 65568 | tf_op jit(solution)/shard_map/ppermute | solution.py:37
  89.9 1.7 %finish.1 = (bf16[64,2048]{1,0:T(8,128)(2,1)}, bf16[1,1,512,768]{3,2,1,0:T(8,128)(2,1)}) custom-call(s32[8,16]{1,0:T(8,128)S(1)} %copy-done.7, bf16[4,64,768]{2,1,0:T(8,128)(2,1)S(1)} %cache_join.1.own, bf16[4,64,768]{2,1,0:T(8,128)(2,1)S(1)} %collective-permute-done.29.other, bf16[64,512]{1,0:T(8,128)(2,1)S(1)} %get-tuple-element.50.after.r0, ...), custom_call_target="tpu_custom_call" | custom-call | tf_op jit(solution)/shard_map/finish/pallas_call | solution.py:77
  (66 shorter events, 17.6 us)
Async XLA Ops:
  2.2 6.1 %collective-permute-start = (bf16[28,768]{1,0:T(8,128)(2,1)}, bf16[28,768]{1,0:T(8,128)(2,1)S(1)}, u32[]{:S(2)}, u32[]{:S(2)}) collective-permute-start(bf16[28,768]{1,0:T(8,128)(2,1)} %get-tuple-element.29), channel_id=1, source_target_pairs={{0,2},{1,3},{2,0},{3,1},{4,6},{5,7},{6,4},{7,5},{8,10},{9,11},{10,... | collective-permute-start | bytes 129032 | tf_op jit(solution)/shard_map/ppermute | solution.py:37
  3.7 4.6 %collective-permute-start.1 = (bf16[28,768]{1,0:T(8,128)(2,1)}, bf16[28,768]{1,0:T(8,128)(2,1)S(1)}, u32[]{:S(2)}, u32[]{:S(2)}) collective-permute-start(bf16[28,768]{1,0:T(8,128)(2,1)} %get-tuple-element.30), channel_id=1, source_target_pairs={{0,1},{1,2},{2,3},{3,0},{4,5},{5,6},{6,7},{7,4},{8,9},{9,10},{10,1... | collective-permute-start | bytes 129032 | tf_op jit(solution)/shard_map/ppermute | solution.py:37
  5.8 5.5 %collective-permute-start.2 = (bf16[28,768]{1,0:T(8,128)(2,1)}, bf16[28,768]{1,0:T(8,128)(2,1)S(1)}, u32[]{:S(2)}, u32[]{:S(2)}) collective-permute-start(bf16[28,768]{1,0:T(8,128)(2,1)} %get-tuple-element.31), channel_id=1, source_target_pairs={{0,3},{1,0},{2,1},{3,2},{4,7},{5,4},{6,5},{7,6},{8,11},{9,8},{10,9... | collective-permute-start | bytes 129032 | tf_op jit(solution)/shard_map/ppermute | solution.py:37
  11.4 7.9 %collective-permute-start.5 = (bf16[112,768]{1,0:T(8,128)(2,1)S(1)}, bf16[112,768]{1,0:T(8,128)(2,1)S(1)}, u32[]{:S(2)}, u32[]{:S(2)}) collective-permute-start(bf16[112,768]{1,0:T(8,128)(2,1)S(1)} %place.1.after.s0), channel_id=1, source_target_pairs={{0,64},{1,65},{2,66},{3,67},{4,68},{5,69},{6,70},{7,71},{8,72},{9,... | collective-permute-start | bytes 516104 | tf_op jit(solution)/shard_map/ppermute | solution.py:37
  15.4 6.3 %collective-permute-start.6 = (bf16[112,768]{1,0:T(8,128)(2,1)S(1)}, bf16[112,768]{1,0:T(8,128)(2,1)S(1)}, u32[]{:S(2)}, u32[]{:S(2)}) collective-permute-start(bf16[112,768]{1,0:T(8,128)(2,1)S(1)} %place.1.after.s0), channel_id=1, source_target_pairs={{0,96},{1,97},{2,98},{3,99},{4,100},{5,101},{6,102},{7,103},{8,104... | collective-permute-start | bytes 516104 | tf_op jit(solution)/shard_map/ppermute | solution.py:37
  16.1 6.6 %collective-permute-start.7 = (bf16[112,768]{1,0:T(8,128)(2,1)S(1)}, bf16[112,768]{1,0:T(8,128)(2,1)S(1)}, u32[]{:S(2)}, u32[]{:S(2)}) collective-permute-start(bf16[112,768]{1,0:T(8,128)(2,1)S(1)} %place.1.after.s0), channel_id=1, source_target_pairs={{0,32},{1,33},{2,34},{3,35},{4,36},{5,37},{6,38},{7,39},{8,40},{9,... | collective-permute-start | bytes 516104 | tf_op jit(solution)/shard_map/ppermute | solution.py:37
  22.8 13.8 %collective-permute-start.8 = (bf16[4,112,768]{2,1,0:T(8,128)(2,1)S(1)}, bf16[4,112,768]{2,1,0:T(8,128)(2,1)S(1)}, u32[]{:S(2)}, u32[]{:S(2)}) collective-permute-start(bf16[4,112,768]{2,1,0:T(8,128)(2,1)S(1)} %stage.1.s0), channel_id=1, source_target_pairs={{0,12},{1,13},{2,14},{3,15},{4,0},{5,1},{6,2},{7,3},{8,4},{9,5},{1... | collective-permute-start | bytes 2064392 | tf_op jit(solution)/shard_map/ppermute | solution.py:37
  26.0 12.1 %collective-permute-start.9 = (bf16[4,112,768]{2,1,0:T(8,128)(2,1)S(1)}, bf16[4,112,768]{2,1,0:T(8,128)(2,1)S(1)}, u32[]{:S(2)}, u32[]{:S(2)}) collective-permute-start(bf16[4,112,768]{2,1,0:T(8,128)(2,1)S(1)} %stage.1.s0), channel_id=1, source_target_pairs={{0,4},{1,5},{2,6},{3,7},{4,8},{5,9},{6,10},{7,11},{8,12},{9,13},{1... | collective-permute-start | bytes 2064392 | tf_op jit(solution)/shard_map/ppermute | solution.py:37
  26.1 10.6 %collective-permute-start.3 = (bf16[64,3584]{1,0:T(8,128)(2,1)S(1)}, bf16[64,3584]{1,0:T(8,128)(2,1)S(1)}, u32[]{:S(2)}, u32[]{:S(2)}) collective-permute-start(bf16[64,3584]{1,0:T(8,128)(2,1)S(1)} %norm.1.after.n0), channel_id=1, source_target_pairs={{0,3},{1,0},{2,1},{3,2},{4,7},{5,4},{6,5},{7,6},{8,11},{9,8},{10,9... | collective-permute-start | bytes 1376264 | tf_op jit(solution)/shard_map/ppermute | solution.py:37
  26.1 10.6 %collective-permute-start.4 = (bf16[64,3584]{1,0:T(8,128)(2,1)S(1)}, bf16[64,3584]{1,0:T(8,128)(2,1)S(1)}, u32[]{:S(2)}, u32[]{:S(2)}) collective-permute-start(bf16[64,3584]{1,0:T(8,128)(2,1)S(1)} %norm.1.after.n0), channel_id=1, source_target_pairs={{0,1},{1,2},{2,3},{3,0},{4,5},{5,6},{6,7},{7,4},{8,9},{9,10},{10,1... | collective-permute-start | bytes 1376264 | tf_op jit(solution)/shard_map/ppermute | solution.py:37
  38.4 10.9 %collective-permute-start.14 = (bf16[12,112,768]{2,1,0:T(8,128)(2,1)S(1)}, bf16[12,112,768]{2,1,0:T(8,128)(2,1)S(1)}, u32[]{:S(2)}, u32[]{:S(2)}) collective-permute-start(bf16[12,112,768]{2,1,0:T(8,128)(2,1)S(1)} %get-tuple-element.32.own1), channel_id=1, source_target_pairs={{0,16},{1,17},{2,18},{3,19},{4,20},{5,21},{6,22},{7,23},{8,24},{9,... | collective-permute-start | bytes 6193160 | tf_op jit(solution)/shard_map/ppermute | solution.py:37
  38.5 10.7 %collective-permute-start.12 = (bf16[2,112,768]{2,1,0:T(8,128)(2,1)S(1)}, bf16[2,112,768]{2,1,0:T(8,128)(2,1)S(1)}, u32[]{:S(2)}, u32[]{:S(2)}) collective-permute-start(bf16[2,112,768]{2,1,0:T(8,128)(2,1)S(1)} %get-tuple-element.35), channel_id=1, source_target_pairs={{0,12},{1,13},{2,14},{3,15},{4,0},{5,1},{6,2},{7,3},{8,4},{9,5},{1... | collective-permute-start | bytes 1032200 | tf_op jit(solution)/shard_map/ppermute | solution.py:37
  39.4 9.8 %collective-permute-start.13 = (bf16[2,112,768]{2,1,0:T(8,128)(2,1)S(1)}, bf16[2,112,768]{2,1,0:T(8,128)(2,1)S(1)}, u32[]{:S(2)}, u32[]{:S(2)}) collective-permute-start(bf16[2,112,768]{2,1,0:T(8,128)(2,1)S(1)} %get-tuple-element.36), channel_id=1, source_target_pairs={{0,4},{1,5},{2,6},{3,7},{4,8},{5,9},{6,10},{7,11},{8,12},{9,13},{1... | collective-permute-start | bytes 1032200 | tf_op jit(solution)/shard_map/ppermute | solution.py:37
  40.6 8.6 %collective-permute-start.10 = (bf16[32,3584]{1,0:T(8,128)(2,1)S(1)}, bf16[32,3584]{1,0:T(8,128)(2,1)S(1)}, u32[]{:S(2)}, u32[]{:S(2)}) collective-permute-start(bf16[32,3584]{1,0:T(8,128)(2,1)S(1)} %get-tuple-element.33), channel_id=1, source_target_pairs={{0,3},{1,0},{2,1},{3,2},{4,7},{5,4},{6,5},{7,6},{8,11},{9,8},{10,9... | collective-permute-start | bytes 688136 | tf_op jit(solution)/shard_map/ppermute | solution.py:37
  40.6 8.6 %collective-permute-start.11 = (bf16[32,3584]{1,0:T(8,128)(2,1)S(1)}, bf16[32,3584]{1,0:T(8,128)(2,1)S(1)}, u32[]{:S(2)}, u32[]{:S(2)}) collective-permute-start(bf16[32,3584]{1,0:T(8,128)(2,1)S(1)} %get-tuple-element.34), channel_id=1, source_target_pairs={{0,1},{1,2},{2,3},{3,0},{4,5},{5,6},{6,7},{7,4},{8,9},{9,10},{10,1... | collective-permute-start | bytes 688136 | tf_op jit(solution)/shard_map/ppermute | solution.py:37
  52.3 6.4 %collective-permute-start.17 = (bf16[256,256]{1,0:T(8,128)(2,1)S(1)}, bf16[256,256]{1,0:T(8,128)(2,1)S(1)}, u32[]{:S(2)}, u32[]{:S(2)}) collective-permute-start(bf16[256,256]{1,0:T(8,128)(2,1)S(1)} %get-tuple-element.41.a0), channel_id=1, source_target_pairs={{0,12},{1,13},{2,14},{3,15},{4,0},{5,1},{6,2},{7,3},{8,4},{9,5},{1... | collective-permute-start | bytes 393224 | tf_op jit(solution)/shard_map/ppermute | solution.py:37
  53.5 7.9 %collective-permute-start.16 = (bf16[256,256]{1,0:T(8,128)(2,1)S(1)}, bf16[256,256]{1,0:T(8,128)(2,1)S(1)}, u32[]{:S(2)}, u32[]{:S(2)}) collective-permute-start(bf16[256,256]{1,0:T(8,128)(2,1)S(1)} %get-tuple-element.41.a0), channel_id=1, source_target_pairs={{0,8},{1,9},{2,10},{3,11},{4,12},{5,13},{6,14},{7,15},{8,0},{9,1},... | collective-permute-start | bytes 393224 | tf_op jit(solution)/shard_map/ppermute | solution.py:37
  54.2 8.8 %collective-permute-start.18 = (bf16[256,256]{1,0:T(8,128)(2,1)S(1)}, bf16[256,256]{1,0:T(8,128)(2,1)S(1)}, u32[]{:S(2)}, u32[]{:S(2)}) collective-permute-start(bf16[256,256]{1,0:T(8,128)(2,1)S(1)} %get-tuple-element.41.a0), channel_id=1, source_target_pairs={{0,4},{1,5},{2,6},{3,7},{4,8},{5,9},{6,10},{7,11},{8,12},{9,13},{1... | collective-permute-start | bytes 393224 | tf_op jit(solution)/shard_map/ppermute | solution.py:37
  55.1 8.0 %collective-permute-start.19 = (bf16[256,256]{1,0:T(8,128)(2,1)S(1)}, bf16[256,256]{1,0:T(8,128)(2,1)S(1)}, u32[]{:S(2)}, u32[]{:S(2)}) collective-permute-start(bf16[256,256]{1,0:T(8,128)(2,1)S(1)} %get-tuple-element.41.a0), channel_id=1, source_target_pairs={{0,1},{1,0},{2,3},{3,2},{4,5},{5,4},{6,7},{7,6},{8,9},{9,8},{10,11... | collective-permute-start | bytes 393224 | tf_op jit(solution)/shard_map/ppermute | solution.py:37
  58.7 16.7 %collective-permute-start.26 = (bf16[256,256]{1,0:T(8,128)(2,1)S(1)}, bf16[256,256]{1,0:T(8,128)(2,1)S(1)}, u32[]{:S(2)}, u32[]{:S(2)}) collective-permute-start(bf16[256,256]{1,0:T(8,128)(2,1)S(1)} %collective-permute-done.17.a1), channel_id=1, source_target_pairs={{0,1},{1,0},{2,3},{3,2},{4,5},{5,4},{6,7},{7,6},{8,9},{9,8},{10,11... | collective-permute-start | bytes 393224 | tf_op jit(solution)/shard_map/ppermute | solution.py:37
  63.2 5.9 %collective-permute-start.20 = (bf16[64,256]{1,0:T(8,128)(2,1)S(1)}, bf16[64,256]{1,0:T(8,128)(2,1)S(1)}, u32[]{:S(2)}, u32[]{:S(2)}) collective-permute-start(bf16[64,256]{1,0:T(8,128)(2,1)S(1)} %get-tuple-element.45), channel_id=1, source_target_pairs={{0,2},{1,3},{2,0},{3,1},{4,6},{5,7},{6,4},{7,5},{8,10},{9,11},{10,... | collective-permute-start | bytes 98312 | tf_op jit(solution)/shard_map/ppermute | solution.py:37
  66.3 4.1 %collective-permute-start.21 = (bf16[64,256]{1,0:T(8,128)(2,1)S(1)}, bf16[64,256]{1,0:T(8,128)(2,1)S(1)}, u32[]{:S(2)}, u32[]{:S(2)}) collective-permute-start(bf16[64,256]{1,0:T(8,128)(2,1)S(1)} %get-tuple-element.46), channel_id=1, source_target_pairs={{0,1},{1,2},{2,3},{3,0},{4,5},{5,6},{6,7},{7,4},{8,9},{9,10},{10,1... | collective-permute-start | bytes 98312 | tf_op jit(solution)/shard_map/ppermute | solution.py:37
  67.1 5.1 %collective-permute-start.22 = (bf16[64,256]{1,0:T(8,128)(2,1)S(1)}, bf16[64,256]{1,0:T(8,128)(2,1)S(1)}, u32[]{:S(2)}, u32[]{:S(2)}) collective-permute-start(bf16[64,256]{1,0:T(8,128)(2,1)S(1)} %get-tuple-element.47), channel_id=1, source_target_pairs={{0,3},{1,0},{2,1},{3,2},{4,7},{5,4},{6,5},{7,6},{8,11},{9,8},{10,9... | collective-permute-start | bytes 98312 | tf_op jit(solution)/shard_map/ppermute | solution.py:37
  68.3 9.1 %collective-permute-start.27 = (bf16[256,256]{1,0:T(8,128)(2,1)S(1)}, bf16[256,256]{1,0:T(8,128)(2,1)S(1)}, u32[]{:S(2)}, u32[]{:S(2)}) collective-permute-start(bf16[256,256]{1,0:T(8,128)(2,1)S(1)} %collective-permute-done.16.a2), channel_id=1, source_target_pairs={{0,1},{1,0},{2,3},{3,2},{4,5},{5,4},{6,7},{7,6},{8,9},{9,8},{10,11... | collective-permute-start | bytes 393224 | tf_op jit(solution)/shard_map/ppermute | solution.py:37
  69.2 8.3 %collective-permute-start.28 = (bf16[256,256]{1,0:T(8,128)(2,1)S(1)}, bf16[256,256]{1,0:T(8,128)(2,1)S(1)}, u32[]{:S(2)}, u32[]{:S(2)}) collective-permute-start(bf16[256,256]{1,0:T(8,128)(2,1)S(1)} %collective-permute-done.18.a3), channel_id=1, source_target_pairs={{0,1},{1,0},{2,3},{3,2},{4,5},{5,4},{6,7},{7,6},{8,9},{9,8},{10,11... | collective-permute-start | bytes 393224 | tf_op jit(solution)/shard_map/ppermute | solution.py:37
  72.3 6.9 %collective-permute-start.23 = (bf16[64,768]{1,0:T(8,128)(2,1)S(1)}, bf16[64,768]{1,0:T(8,128)(2,1)S(1)}, u32[]{:S(2)}, u32[]{:S(2)}) collective-permute-start(bf16[64,768]{1,0:T(8,128)(2,1)S(1)} %cache_heads.1.after.c0), channel_id=1, source_target_pairs={{0,64},{1,65},{2,66},{3,67},{4,68},{5,69},{6,70},{7,71},{8,72},{9,... | collective-permute-start | bytes 294920 | tf_op jit(solution)/shard_map/ppermute | solution.py:37
  73.8 6.0 %collective-permute-start.24 = (bf16[64,768]{1,0:T(8,128)(2,1)S(1)}, bf16[64,768]{1,0:T(8,128)(2,1)S(1)}, u32[]{:S(2)}, u32[]{:S(2)}) collective-permute-start(bf16[64,768]{1,0:T(8,128)(2,1)S(1)} %cache_heads.1.after.c0), channel_id=1, source_target_pairs={{0,96},{1,97},{2,98},{3,99},{4,100},{5,101},{6,102},{7,103},{8,104... | collective-permute-start | bytes 294920 | tf_op jit(solution)/shard_map/ppermute | solution.py:37
  75.4 5.8 %collective-permute-start.25 = (bf16[64,768]{1,0:T(8,128)(2,1)S(1)}, bf16[64,768]{1,0:T(8,128)(2,1)S(1)}, u32[]{:S(2)}, u32[]{:S(2)}) collective-permute-start(bf16[64,768]{1,0:T(8,128)(2,1)S(1)} %cache_heads.1.after.c0), channel_id=1, source_target_pairs={{0,32},{1,33},{2,34},{3,35},{4,36},{5,37},{6,38},{7,39},{8,40},{9,... | collective-permute-start | bytes 294920 | tf_op jit(solution)/shard_map/ppermute | solution.py:37
  81.2 8.6 %collective-permute-start.29 = (bf16[4,64,768]{2,1,0:T(8,128)(2,1)S(1)}, bf16[4,64,768]{2,1,0:T(8,128)(2,1)S(1)}, u32[]{:S(2)}, u32[]{:S(2)}) collective-permute-start(bf16[4,64,768]{2,1,0:T(8,128)(2,1)S(1)} %cache_join.1.own), channel_id=1, source_target_pairs={{0,16},{1,17},{2,18},{3,19},{4,20},{5,21},{6,22},{7,23},{8,24},{9,... | collective-permute-start | bytes 1179656 | tf_op jit(solution)/shard_map/ppermute | solution.py:37
  81.3 6.0 %collective-permute-start.30 = (bf16[64,512]{1,0:T(8,128)(2,1)S(1)}, bf16[64,512]{1,0:T(8,128)(2,1)S(1)}, u32[]{:S(2)}, u32[]{:S(2)}) collective-permute-start(bf16[64,512]{1,0:T(8,128)(2,1)S(1)} %get-tuple-element.51), channel_id=1, source_target_pairs={{0,2},{1,3},{2,0},{3,1},{4,6},{5,7},{6,4},{7,5},{8,10},{9,11},{10,... | collective-permute-start | bytes 196616 | tf_op jit(solution)/shard_map/ppermute | solution.py:37
  82.6 4.7 %collective-permute-start.31 = (bf16[64,512]{1,0:T(8,128)(2,1)S(1)}, bf16[64,512]{1,0:T(8,128)(2,1)S(1)}, u32[]{:S(2)}, u32[]{:S(2)}) collective-permute-start(bf16[64,512]{1,0:T(8,128)(2,1)S(1)} %get-tuple-element.52), channel_id=1, source_target_pairs={{0,1},{1,2},{2,3},{3,0},{4,5},{5,6},{6,7},{7,4},{8,9},{9,10},{10,1... | collective-permute-start | bytes 196616 | tf_op jit(solution)/shard_map/ppermute | solution.py:37
  84.4 5.5 %collective-permute-start.32 = (bf16[64,512]{1,0:T(8,128)(2,1)S(1)}, bf16[64,512]{1,0:T(8,128)(2,1)S(1)}, u32[]{:S(2)}, u32[]{:S(2)}) collective-permute-start(bf16[64,512]{1,0:T(8,128)(2,1)S(1)} %get-tuple-element.53), channel_id=1, source_target_pairs={{0,3},{1,0},{2,1},{3,2},{4,7},{5,4},{6,5},{7,6},{8,11},{9,8},{10,9... | collective-permute-start | bytes 196616 | tf_op jit(solution)/shard_map/ppermute | solution.py:37
  (9 other events, 128.8 us)
where the time goes:
time: 91.8 us; the launch traced here: 91.5 us
  starting transfers between devices  40.7 us (44%)
  waiting for transfers between devices  36.7 us (40%)
  Pallas kernels  10.7 us (12%)
  local copies, waits for them, and re-layouts  2.57 us (3%)
    ppermute x33, starting transfers between devices, send(): return lax.ppermute(v, EVERY, [(flat(*p), flat(*move(*p))) for p in PLACES])  40.7 us
    ppermute x33, waiting for transfers between devices, send(): return lax.ppermute(v, EVERY, [(flat(*p), flat(*move(*p))) for p in PLACES])  36.7 us
    pallas_call x16, Pallas kernels, call(): pl.pallas_call(kernel, out_shape=outs, in_specs=[VM] * len(operands) if i...  10.7 us
    unnamed x16, local copies, waits for them, and re-layouts  2.57 us
  transfers between devices with their start and end apart: 33, of which 16 were waited for; matrix products, arithmetic and copies ran while one was open for 0% of the time, Pallas kernels for 7%

commit v1 on v0

--- a/solution.py
+++ b/solution.py
@@ -41,7 +41,12 @@
     return [one(j) for j in (2, 1, 3)]
 
 
+def spread_down(one):
+    return [one(j) for j in (2, 3, 1)]
+
+
 HOPS = (0, 2, 1, 3)
+DOWN = (0, 2, 3, 1)
 
 
 def along_x(j):
@@ -124,7 +129,7 @@
     out[...] = jnp.concatenate([buf[k] for k in range(4)], axis=0).astype(jnp.bfloat16)
 
 
-def stage(s0, s2, s1, s3, after, block):
+def stage(s0, s2, s3, s1, after, block):
     for i, s in enumerate((s0, s1, s2, s3)):
         block[i] = s[...]
 
@@ -262,7 +267,7 @@
     last[...] = one_head(q[:, 3 * HEAD :], [a[...] for a in (a0, a1, a2, a3)], mask)
 
 
-def attend(mask, last, q, a0, a1, a2, a3, b0, b1, b2, b3, o0, o1, o2, o3, full):
+def attend(mask, last, q, a0, a1, a2, a3, b0, b3, b2, b1, o0, o1, o2, o3, full):
     x = lax.axis_index("x")
     for h in range(3):
         left = (x == 1) if h == 2 else ((x == 1) | (x == 3))
@@ -278,14 +283,14 @@
         o[...] = full[pl.ds(pl.multiple_of(lax.rem(x + j, 4) * 64, 64), 64), :]
 
 
-def cache_rows(a0, a2, a1, a3, after1, after2, t0, t1, t2, t3):
+def cache_rows(a0, a2, a3, a1, after1, after2, t0, t1, t2, t3):
     x = lax.axis_index("x")
     y = lax.axis_index("y")
     i = lax.broadcasted_iota(jnp.int32, (64, ROW_TOK), 0)
     t = lax.broadcasted_iota(jnp.int32, (64, ROW_TOK), 1)
     want = 16 * lax.rem(i, 16) + 4 * y + lax.rem(x + lax.div(i, 16), 4)
     select = jnp.where(t == want, 1.0, 0.0).astype(jnp.bfloat16)
-    for j, a in zip(HOPS, (a0, a2, a1, a3)):
+    for j, a in zip(DOWN, (a0, a2, a3, a1)):
         got = jnp.dot(select, a[...], preferred_element_type=jnp.float32).astype(jnp.bfloat16)
         rows = pl.ds(pl.multiple_of(lax.rem(y + j, 4) * 16, 16), 16)
         for k, out in enumerate((t0, t1, t2, t3)):
@@ -301,8 +306,8 @@
         out[:, (3 + k) * HEAD : (4 + k) * HEAD] = buf[src, :, HEAD:]
 
 
-def cache_join(c0, c2, c1, c3, after, out):
-    for n, c in zip(HOPS, (c0, c2, c1, c3)):
+def cache_join(c0, c2, c3, c1, after, out):
+    for n, c in zip(DOWN, (c0, c2, c3, c1)):
         out[n] = c[...]
 
 
@@ -344,7 +349,7 @@
     (s0,) = call(
         stage,
         [((4, 112, COLS), bf)],
-        (w0, *spread(lambda j: send(w0, along_first(-j))), n0),
+        (w0, *spread_down(lambda j: send(w0, along_first(-j))), n0),
         [VM] * 4 + [ANY],
     )
     n1 = send(n0, along_x(-1))
@@ -389,10 +394,10 @@
     )
     (q,) = call(q_project, [((ROW_TOK, 512), bf)], (w, x_all, cs, qb))
 
-    a2, a1, a3 = spread(lambda j: send(kv, along_y(-j)))
+    a2, a3, a1 = spread_down(lambda j: send(kv, along_y(-j)))
     a = [kv, a1, a2, a3]
     b = [send(v, pair_x) for v in a]
-    rows = call(cache_rows, [((64, 256), bf)] * 4, (kv, a2, a1, a3, q, b[0]), [VM] * 4 + [ANY] * 2)
+    rows = call(cache_rows, [((64, 256), bf)] * 4, (kv, a2, a3, a1, q, b[0]), [VM] * 4 + [ANY] * 2)
     (mine,) = call(
         cache_heads,
         [((64, 768), bf)],
@@ -408,13 +413,13 @@
     outs = call(
         attend,
         [((64, 512), bf)] * 4,
-        (mask, last, q, *a, *b),
+        (mask, last, q, *a, b[0], b[3], b[2], b[1]),
         scratch=[pltpu.VMEM((ROW_TOK, 512), bf)],
     )
     (cached,) = call(
         cache_join,
         [((4, 64, 768), bf)],
-        (mine, *spread(lambda j: send(mine, along_z(-j))), outs[0]),
+        (mine, *spread_down(lambda j: send(mine, along_z(-j))), outs[0]),
         [VM] * 4 + [ANY],
     )
     attended, cache = call(

time: 91.8 us -> 93.4 us (1.017)
  starting transfers between devices: 40.7 us -> 43.4 us
  waiting for transfers between devices: 36.7 us -> 35.6 us
    ppermute x33, starting transfers between devices: 40.7 us -> 43.4 us  [send(): return lax.ppermute(v, EVERY, [(flat(*p), flat(*move(*p))) for p in PLACES])]
    ppermute x33, waiting for transfers between devices: 36.7 us -> 35.6 us  [send(): return lax.ppermute(v, EVERY, [(flat(*p), flat(*move(*p))) for p in PLACES])]
  transfers between devices with their start and end apart: 33 -> 33, of which waited for: 16 -> 14; matrix products, arithmetic and copies ran while one was open for 0% -> 0% of each run, Pallas kernels for 7% -> 7%
where the time goes in v1:
time: 93.4 us; the launch traced here: 93.2 us
  starting transfers between devices  43.4 us (46%)
  waiting for transfers between devices  35.6 us (38%)
  Pallas kernels  10.7 us (11%)
  local copies, waits for them, and re-layouts  2.57 us (3%)
    ppermute x33, starting transfers between devices, send(): return lax.ppermute(v, EVERY, [(flat(*p), flat(*move(*p))) for p in PLACES])  43.4 us
    ppermute x33, waiting for transfers between devices, send(): return lax.ppermute(v, EVERY, [(flat(*p), flat(*move(*p))) for p in PLACES])  35.6 us
    pallas_call x16, Pallas kernels, call(): pl.pallas_call(kernel, out_shape=outs, in_specs=[VM] * len(operands) if i...  10.7 us
    unnamed x16, local copies, waits for them, and re-layouts  2.57 us
  transfers between devices with their start and end apart: 33, of which 14 were waited for; matrix products, arithmetic and copies ran while one was open for 0% of the time, Pallas kernels for 7%

profile of v1, /device:TPU:6, one launch (start us, length us, event | category | flops | bytes accessed | tf_op | source)
XLA Modules:
  0.0 93.2 jit_solution(8005454616852785368)
XLA Ops:
  0.6 1.6 %cut.1 = (bf16[28,768]{1,0:T(8,128)(2,1)}, bf16[28,768]{1,0:T(8,128)(2,1)}, bf16[28,768]{1,0:T(8,128)(2,1)}, bf16[28,768]{1,0:T(8,128)(2,1)}) custom-call(bf16[28,2048]{1,0:T(8,128)(2,1)} %wq.1, bf16[28,768]{1,0:T(8,128)(2,1)} %wkv.1), custom_call_target="tpu_custom_call" | custom-call | tf_op jit(solution)/shard_map/cut/pallas_call | solution.py:82
  2.2 1.5 %collective-permute-start = (bf16[28,768]{1,0:T(8,128)(2,1)}, bf16[28,768]{1,0:T(8,128)(2,1)S(1)}, u32[]{:S(2)}, u32[]{:S(2)}) collective-permute-start(bf16[28,768]{1,0:T(8,128)(2,1)} %get-tuple-element.29), channel_id=1, source_target_pairs={{0,2},{1,3},{2,0},{3,1},{4,6},{5,7},{6,4},{7,5},{8,10},{9,11},{10,... | collective-permute-start | bytes 129032 | tf_op jit(solution)/shard_map/ppermute | solution.py:37
  3.7 2.1 %collective-permute-start.1 = (bf16[28,768]{1,0:T(8,128)(2,1)}, bf16[28,768]{1,0:T(8,128)(2,1)S(1)}, u32[]{:S(2)}, u32[]{:S(2)}) collective-permute-start(bf16[28,768]{1,0:T(8,128)(2,1)} %get-tuple-element.30), channel_id=1, source_target_pairs={{0,1},{1,2},{2,3},{3,0},{4,5},{5,6},{6,7},{7,4},{8,9},{9,10},{10,1... | collective-permute-start | bytes 129032 | tf_op jit(solution)/shard_map/ppermute | solution.py:37
  6.7 1.6 %collective-permute-done.p2 = bf16[28,768]{1,0:T(8,128)(2,1)S(1)} collective-permute-done((bf16[28,768]{1,0:T(8,128)(2,1)}, bf16[28,768]{1,0:T(8,128)(2,1)S(1)}, u32[]{:S(2)}, u32[]{:S(2)}) %collective-permute-start) | collective-permute-done | bytes 43040 | tf_op jit(solution)/shard_map/ppermute | solution.py:37
  8.3 3.0 %collective-permute-done.2.p3 = bf16[28,768]{1,0:T(8,128)(2,1)S(1)} collective-permute-done((bf16[28,768]{1,0:T(8,128)(2,1)}, bf16[28,768]{1,0:T(8,128)(2,1)S(1)}, u32[]{:S(2)}, u32[]{:S(2)}) %collective-permute-start.2) | collective-permute-done | bytes 43040 | tf_op jit(solution)/shard_map/ppermute | solution.py:37
  11.4 4.0 %collective-permute-start.5 = (bf16[112,768]{1,0:T(8,128)(2,1)S(1)}, bf16[112,768]{1,0:T(8,128)(2,1)S(1)}, u32[]{:S(2)}, u32[]{:S(2)}) collective-permute-start(bf16[112,768]{1,0:T(8,128)(2,1)S(1)} %place.1.after.s0), channel_id=1, source_target_pairs={{0,64},{1,65},{2,66},{3,67},{4,68},{5,69},{6,70},{7,71},{8,72},{9,... | collective-permute-start | bytes 516104 | tf_op jit(solution)/shard_map/ppermute | solution.py:37
  15.4 1.0 %collective-permute-start.6 = (bf16[112,768]{1,0:T(8,128)(2,1)S(1)}, bf16[112,768]{1,0:T(8,128)(2,1)S(1)}, u32[]{:S(2)}, u32[]{:S(2)}) collective-permute-start(bf16[112,768]{1,0:T(8,128)(2,1)S(1)} %place.1.after.s0), channel_id=1, source_target_pairs={{0,32},{1,33},{2,34},{3,35},{4,36},{5,37},{6,38},{7,39},{8,40},{9,... | collective-permute-start | bytes 516104 | tf_op jit(solution)/shard_map/ppermute | solution.py:37
  16.4 2.2 %collective-permute-start.7 = (bf16[112,768]{1,0:T(8,128)(2,1)S(1)}, bf16[112,768]{1,0:T(8,128)(2,1)S(1)}, u32[]{:S(2)}, u32[]{:S(2)}) collective-permute-start(bf16[112,768]{1,0:T(8,128)(2,1)S(1)} %place.1.after.s0), channel_id=1, source_target_pairs={{0,96},{1,97},{2,98},{3,99},{4,100},{5,101},{6,102},{7,103},{8,104... | collective-permute-start | bytes 516104 | tf_op jit(solution)/shard_map/ppermute | solution.py:37
  20.6 1.4 %collective-permute-done.6.s3 = bf16[112,768]{1,0:T(8,128)(2,1)S(1)} collective-permute-done((bf16[112,768]{1,0:T(8,128)(2,1)S(1)}, bf16[112,768]{1,0:T(8,128)(2,1)S(1)}, u32[]{:S(2)}, u32[]{:S(2)}) %collective-permute-start.6) | collective-permute-done | bytes 172064 | tf_op jit(solution)/shard_map/ppermute | solution.py:37
  22.6 3.2 %collective-permute-start.8 = (bf16[4,112,768]{2,1,0:T(8,128)(2,1)S(1)}, bf16[4,112,768]{2,1,0:T(8,128)(2,1)S(1)}, u32[]{:S(2)}, u32[]{:S(2)}) collective-permute-start(bf16[4,112,768]{2,1,0:T(8,128)(2,1)S(1)} %stage.1.s0), channel_id=1, source_target_pairs={{0,12},{1,13},{2,14},{3,15},{4,0},{5,1},{6,2},{7,3},{8,4},{9,5},{1... | collective-permute-start | bytes 2064392 | tf_op jit(solution)/shard_map/ppermute | solution.py:37
  25.7 3.2 %collective-permute-start.4 = (bf16[64,3584]{1,0:T(8,128)(2,1)S(1)}, bf16[64,3584]{1,0:T(8,128)(2,1)S(1)}, u32[]{:S(2)}, u32[]{:S(2)}) collective-permute-start(bf16[64,3584]{1,0:T(8,128)(2,1)S(1)} %norm.1.after.n0), channel_id=1, source_target_pairs={{0,1},{1,2},{2,3},{3,0},{4,5},{5,6},{6,7},{7,4},{8,9},{9,10},{10,1... | collective-permute-start | bytes 1376264 | tf_op jit(solution)/shard_map/ppermute | solution.py:37
  29.0 6.9 %collective-permute-done.3.n1 = bf16[64,3584]{1,0:T(8,128)(2,1)S(1)} collective-permute-done((bf16[64,3584]{1,0:T(8,128)(2,1)S(1)}, bf16[64,3584]{1,0:T(8,128)(2,1)S(1)}, u32[]{:S(2)}, u32[]{:S(2)}) %collective-permute-start.3) | collective-permute-done | bytes 458784 | tf_op jit(solution)/shard_map/ppermute | solution.py:37
  35.9 2.0 %collective-permute-done.9.s3 = bf16[4,112,768]{2,1,0:T(8,128)(2,1)S(1)} collective-permute-done((bf16[4,112,768]{2,1,0:T(8,128)(2,1)S(1)}, bf16[4,112,768]{2,1,0:T(8,128)(2,1)S(1)}, u32[]{:S(2)}, u32[]{:S(2)}) %collective-permute-start.9) | collective-permute-done | bytes 688160 | tf_op jit(solution)/shard_map/ppermute | solution.py:37
  39.2 1.1 %collective-permute-start.13 = (bf16[2,112,768]{2,1,0:T(8,128)(2,1)S(1)}, bf16[2,112,768]{2,1,0:T(8,128)(2,1)S(1)}, u32[]{:S(2)}, u32[]{:S(2)}) collective-permute-start(bf16[2,112,768]{2,1,0:T(8,128)(2,1)S(1)} %get-tuple-element.36), channel_id=1, source_target_pairs={{0,4},{1,5},{2,6},{3,7},{4,8},{5,9},{6,10},{7,11},{8,12},{9,13},{1... | collective-permute-start | bytes 1032200 | tf_op jit(solution)/shard_map/ppermute | solution.py:37
  40.3 3.2 %collective-permute-start.11 = (bf16[32,3584]{1,0:T(8,128)(2,1)S(1)}, bf16[32,3584]{1,0:T(8,128)(2,1)S(1)}, u32[]{:S(2)}, u32[]{:S(2)}) collective-permute-start(bf16[32,3584]{1,0:T(8,128)(2,1)S(1)} %get-tuple-element.34), channel_id=1, source_target_pairs={{0,1},{1,2},{2,3},{3,0},{4,5},{5,6},{6,7},{7,4},{8,9},{9,10},{10,1... | collective-permute-start | bytes 688136 | tf_op jit(solution)/shard_map/ppermute | solution.py:37
  43.5 6.3 %collective-permute-done.10.after1.n2a = bf16[32,3584]{1,0:T(8,128)(2,1)S(1)} collective-permute-done((bf16[32,3584]{1,0:T(8,128)(2,1)S(1)}, bf16[32,3584]{1,0:T(8,128)(2,1)S(1)}, u32[]{:S(2)}, u32[]{:S(2)}) %collective-permute-start.10) | collective-permute-done | bytes 229408 | tf_op jit(solution)/shard_map/ppermute | solution.py:37
  50.0 1.4 %gather.1 = (bf16[32,112,768]{2,1,0:T(8,128)(2,1)S(1)}, bf16[256,3584]{1,0:T(8,128)(2,1)S(1)}, f32[256,128]{1,0:T(8,128)S(1)}, f32[512]{0:T(512)S(1)}, f32[2,128]{1,0:T(2,128)S(1)}) custom-call(s32[8,16]{1,0:T(8,128)S(1)} %copy-done.3, bf16[12,112,768]{2,1,0:T(8,128)(2,1)S(1)} %get-tuple-element.32.own1, bf16[4,112,768]{2,1,0:T(8,128)(2,1)S(1)} %join2.1.own2, ...), custom_call_target="tpu_custom_call" | custom-call | tf_op jit(solution)/shard_map/gather/pallas_call | solution.py:82
  52.9 2.7 %collective-permute-start.16 = (bf16[256,256]{1,0:T(8,128)(2,1)S(1)}, bf16[256,256]{1,0:T(8,128)(2,1)S(1)}, u32[]{:S(2)}, u32[]{:S(2)}) collective-permute-start(bf16[256,256]{1,0:T(8,128)(2,1)S(1)} %get-tuple-element.41.a0), channel_id=1, source_target_pairs={{0,8},{1,9},{2,10},{3,11},{4,12},{5,13},{6,14},{7,15},{8,0},{9,1},... | collective-permute-start | bytes 393224 | tf_op jit(solution)/shard_map/ppermute | solution.py:37
  57.2 5.3 %collective-permute-done.17.a3 = bf16[256,256]{1,0:T(8,128)(2,1)S(1)} collective-permute-done((bf16[256,256]{1,0:T(8,128)(2,1)S(1)}, bf16[256,256]{1,0:T(8,128)(2,1)S(1)}, u32[]{:S(2)}, u32[]{:S(2)}) %collective-permute-start.17) | collective-permute-done | bytes 131104 | tf_op jit(solution)/shard_map/ppermute | solution.py:37
  62.5 1.4 %q_project.1.after1.q = bf16[256,512]{1,0:T(8,128)(2,1)S(1)} custom-call(bf16[32,112,768]{2,1,0:T(8,128)(2,1)S(1)} %get-tuple-element.42.w, bf16[256,3584]{1,0:T(8,128)(2,1)S(1)} %get-tuple-element.38.x_in, f32[256,128]{1,0:T(8,128)S(1)} %get-tuple-element.39.cs, f32[512]{0:T(512)S(1)} %get-tuple-element.43.qb), custom_call_target="tpu_custom_call" | custom-call | tf_op jit(solution)/shard_map/q_project/pallas_call | solution.py:82
  64.1 4.5 %collective-permute-start.20 = (bf16[64,256]{1,0:T(8,128)(2,1)S(1)}, bf16[64,256]{1,0:T(8,128)(2,1)S(1)}, u32[]{:S(2)}, u32[]{:S(2)}) collective-permute-start(bf16[64,256]{1,0:T(8,128)(2,1)S(1)} %get-tuple-element.45), channel_id=1, source_target_pairs={{0,2},{1,3},{2,0},{3,1},{4,6},{5,7},{6,4},{7,5},{8,10},{9,11},{10,... | collective-permute-start | bytes 98312 | tf_op jit(solution)/shard_map/ppermute | solution.py:37
  68.9 1.7 %collective-permute-start.22 = (bf16[64,256]{1,0:T(8,128)(2,1)S(1)}, bf16[64,256]{1,0:T(8,128)(2,1)S(1)}, u32[]{:S(2)}, u32[]{:S(2)}) collective-permute-start(bf16[64,256]{1,0:T(8,128)(2,1)S(1)} %get-tuple-element.47), channel_id=1, source_target_pairs={{0,3},{1,0},{2,1},{3,2},{4,7},{5,4},{6,5},{7,6},{8,11},{9,8},{10,9... | collective-permute-start | bytes 98312 | tf_op jit(solution)/shard_map/ppermute | solution.py:37
  70.8 1.8 %collective-permute-start.28 = (bf16[256,256]{1,0:T(8,128)(2,1)S(1)}, bf16[256,256]{1,0:T(8,128)(2,1)S(1)}, u32[]{:S(2)}, u32[]{:S(2)}) collective-permute-start(bf16[256,256]{1,0:T(8,128)(2,1)S(1)} %collective-permute-done.18.a1), channel_id=1, source_target_pairs={{0,1},{1,0},{2,3},{3,2},{4,5},{5,4},{6,7},{7,6},{8,9},{9,8},{10,11... | collective-permute-start | bytes 393224 | tf_op jit(solution)/shard_map/ppermute | solution.py:37
  72.7 1.4 %collective-permute-done.22.t3 = bf16[64,256]{1,0:T(8,128)(2,1)S(1)} collective-permute-done((bf16[64,256]{1,0:T(8,128)(2,1)S(1)}, bf16[64,256]{1,0:T(8,128)(2,1)S(1)}, u32[]{:S(2)}, u32[]{:S(2)}) %collective-permute-start.22) | collective-permute-done | bytes 32800 | tf_op jit(solution)/shard_map/ppermute | solution.py:37
  74.1 1.3 %collective-permute-start.23 = (bf16[64,768]{1,0:T(8,128)(2,1)S(1)}, bf16[64,768]{1,0:T(8,128)(2,1)S(1)}, u32[]{:S(2)}, u32[]{:S(2)}) collective-permute-start(bf16[64,768]{1,0:T(8,128)(2,1)S(1)} %cache_heads.1.after.c0), channel_id=1, source_target_pairs={{0,64},{1,65},{2,66},{3,67},{4,68},{5,69},{6,70},{7,71},{8,72},{9,... | collective-permute-start | bytes 294920 | tf_op jit(solution)/shard_map/ppermute | solution.py:37
  75.3 2.4 %collective-permute-start.24 = (bf16[64,768]{1,0:T(8,128)(2,1)S(1)}, bf16[64,768]{1,0:T(8,128)(2,1)S(1)}, u32[]{:S(2)}, u32[]{:S(2)}) collective-permute-start(bf16[64,768]{1,0:T(8,128)(2,1)S(1)} %cache_heads.1.after.c0), channel_id=1, source_target_pairs={{0,32},{1,33},{2,34},{3,35},{4,36},{5,37},{6,38},{7,39},{8,40},{9,... | collective-permute-start | bytes 294920 | tf_op jit(solution)/shard_map/ppermute | solution.py:37
  78.6 1.2 %attend_own.1 = (f32[256,1024]{1,0:T(8,128)S(1)}, bf16[256,128]{1,0:T(8,128)(2,1)S(1)}) custom-call(s32[8,16]{1,0:T(8,128)S(1)} %copy-done.3, bf16[256,512]{1,0:T(8,128)(2,1)S(1)} %q_project.1.after1.q, bf16[256,256]{1,0:T(8,128)(2,1)S(1)} %get-tuple-element.41.a0, bf16[256,256]{1,0:T(8,128)(2,1)S(1)} %collective-permute-done.18.a1, ...), custom_call_target="tpu_custom_call" | custom-call | tf_op jit(solution)/shard_map/attend_own/pallas_call | solution.py:82
  79.9 1.7 %attend.1 = (bf16[64,512]{1,0:T(8,128)(2,1)S(1)}, bf16[64,512]{1,0:T(8,128)(2,1)S(1)}, bf16[64,512]{1,0:T(8,128)(2,1)S(1)}, bf16[64,512]{1,0:T(8,128)(2,1)S(1)}) custom-call(f32[256,1024]{1,0:T(8,128)S(1)} %get-tuple-element.48.mask, bf16[256,128]{1,0:T(8,128)(2,1)S(1)} %get-tuple-element.49.last, bf16[256,512]{1,0:T(8,128)(2,1)S(1)} %q_project.1.after1.q, ...), custom_call_target="tpu_custom_call" | custom-call | tf_op jit(solution)/shard_map/attend/pallas_call | solution.py:82
  83.5 2.5 %collective-permute-start.31 = (bf16[64,512]{1,0:T(8,128)(2,1)S(1)}, bf16[64,512]{1,0:T(8,128)(2,1)S(1)}, u32[]{:S(2)}, u32[]{:S(2)}) collective-permute-start(bf16[64,512]{1,0:T(8,128)(2,1)S(1)} %get-tuple-element.52), channel_id=1, source_target_pairs={{0,1},{1,2},{2,3},{3,0},{4,5},{5,6},{6,7},{7,4},{8,9},{9,10},{10,1... | collective-permute-start | bytes 196616 | tf_op jit(solution)/shard_map/ppermute | solution.py:37
  86.0 2.5 %collective-permute-done.30.r2 = bf16[64,512]{1,0:T(8,128)(2,1)S(1)} collective-permute-done((bf16[64,512]{1,0:T(8,128)(2,1)S(1)}, bf16[64,512]{1,0:T(8,128)(2,1)S(1)}, u32[]{:S(2)}, u32[]{:S(2)}) %collective-permute-start.30) | collective-permute-done | bytes 65568 | tf_op jit(solution)/shard_map/ppermute | solution.py:37
  88.5 3.0 %collective-permute-done.32.r3 = bf16[64,512]{1,0:T(8,128)(2,1)S(1)} collective-permute-done((bf16[64,512]{1,0:T(8,128)(2,1)S(1)}, bf16[64,512]{1,0:T(8,128)(2,1)S(1)}, u32[]{:S(2)}, u32[]{:S(2)}) %collective-permute-start.32) | collective-permute-done | bytes 65568 | tf_op jit(solution)/shard_map/ppermute | solution.py:37
  91.5 1.7 %finish.1 = (bf16[64,2048]{1,0:T(8,128)(2,1)}, bf16[1,1,512,768]{3,2,1,0:T(8,128)(2,1)}) custom-call(s32[8,16]{1,0:T(8,128)S(1)} %copy-done.7, bf16[4,64,768]{2,1,0:T(8,128)(2,1)S(1)} %cache_join.1.own, bf16[4,64,768]{2,1,0:T(8,128)(2,1)S(1)} %collective-permute-done.29.other, bf16[64,512]{1,0:T(8,128)(2,1)S(1)} %get-tuple-element.50.after.r0, ...), custom_call_target="tpu_custom_call" | custom-call | tf_op jit(solution)/shard_map/finish/pallas_call | solution.py:82
  (66 shorter events, 11.4 us)
Async XLA Ops:
  2.2 6.1 %collective-permute-start = (bf16[28,768]{1,0:T(8,128)(2,1)}, bf16[28,768]{1,0:T(8,128)(2,1)S(1)}, u32[]{:S(2)}, u32[]{:S(2)}) collective-permute-start(bf16[28,768]{1,0:T(8,128)(2,1)} %get-tuple-element.29), channel_id=1, source_target_pairs={{0,2},{1,3},{2,0},{3,1},{4,6},{5,7},{6,4},{7,5},{8,10},{9,11},{10,... | collective-permute-start | bytes 129032 | tf_op jit(solution)/shard_map/ppermute | solution.py:37
  3.7 4.6 %collective-permute-start.1 = (bf16[28,768]{1,0:T(8,128)(2,1)}, bf16[28,768]{1,0:T(8,128)(2,1)S(1)}, u32[]{:S(2)}, u32[]{:S(2)}) collective-permute-start(bf16[28,768]{1,0:T(8,128)(2,1)} %get-tuple-element.30), channel_id=1, source_target_pairs={{0,1},{1,2},{2,3},{3,0},{4,5},{5,6},{6,7},{7,4},{8,9},{9,10},{10,1... | collective-permute-start | bytes 129032 | tf_op jit(solution)/shard_map/ppermute | solution.py:37
  5.8 5.5 %collective-permute-start.2 = (bf16[28,768]{1,0:T(8,128)(2,1)}, bf16[28,768]{1,0:T(8,128)(2,1)S(1)}, u32[]{:S(2)}, u32[]{:S(2)}) collective-permute-start(bf16[28,768]{1,0:T(8,128)(2,1)} %get-tuple-element.31), channel_id=1, source_target_pairs={{0,3},{1,0},{2,1},{3,2},{4,7},{5,4},{6,5},{7,6},{8,11},{9,8},{10,9... | collective-permute-start | bytes 129032 | tf_op jit(solution)/shard_map/ppermute | solution.py:37
  11.4 9.1 %collective-permute-start.5 = (bf16[112,768]{1,0:T(8,128)(2,1)S(1)}, bf16[112,768]{1,0:T(8,128)(2,1)S(1)}, u32[]{:S(2)}, u32[]{:S(2)}) collective-permute-start(bf16[112,768]{1,0:T(8,128)(2,1)S(1)} %place.1.after.s0), channel_id=1, source_target_pairs={{0,64},{1,65},{2,66},{3,67},{4,68},{5,69},{6,70},{7,71},{8,72},{9,... | collective-permute-start | bytes 516104 | tf_op jit(solution)/shard_map/ppermute | solution.py:37
  15.4 6.6 %collective-permute-start.6 = (bf16[112,768]{1,0:T(8,128)(2,1)S(1)}, bf16[112,768]{1,0:T(8,128)(2,1)S(1)}, u32[]{:S(2)}, u32[]{:S(2)}) collective-permute-start(bf16[112,768]{1,0:T(8,128)(2,1)S(1)} %place.1.after.s0), channel_id=1, source_target_pairs={{0,32},{1,33},{2,34},{3,35},{4,36},{5,37},{6,38},{7,39},{8,40},{9,... | collective-permute-start | bytes 516104 | tf_op jit(solution)/shard_map/ppermute | solution.py:37
  16.4 6.1 %collective-permute-start.7 = (bf16[112,768]{1,0:T(8,128)(2,1)S(1)}, bf16[112,768]{1,0:T(8,128)(2,1)S(1)}, u32[]{:S(2)}, u32[]{:S(2)}) collective-permute-start(bf16[112,768]{1,0:T(8,128)(2,1)S(1)} %place.1.after.s0), channel_id=1, source_target_pairs={{0,96},{1,97},{2,98},{3,99},{4,100},{5,101},{6,102},{7,103},{8,104... | collective-permute-start | bytes 516104 | tf_op jit(solution)/shard_map/ppermute | solution.py:37
  22.6 13.3 %collective-permute-start.8 = (bf16[4,112,768]{2,1,0:T(8,128)(2,1)S(1)}, bf16[4,112,768]{2,1,0:T(8,128)(2,1)S(1)}, u32[]{:S(2)}, u32[]{:S(2)}) collective-permute-start(bf16[4,112,768]{2,1,0:T(8,128)(2,1)S(1)} %stage.1.s0), channel_id=1, source_target_pairs={{0,12},{1,13},{2,14},{3,15},{4,0},{5,1},{6,2},{7,3},{8,4},{9,5},{1... | collective-permute-start | bytes 2064392 | tf_op jit(solution)/shard_map/ppermute | solution.py:37
  25.7 12.1 %collective-permute-start.9 = (bf16[4,112,768]{2,1,0:T(8,128)(2,1)S(1)}, bf16[4,112,768]{2,1,0:T(8,128)(2,1)S(1)}, u32[]{:S(2)}, u32[]{:S(2)}) collective-permute-start(bf16[4,112,768]{2,1,0:T(8,128)(2,1)S(1)} %stage.1.s0), channel_id=1, source_target_pairs={{0,4},{1,5},{2,6},{3,7},{4,8},{5,9},{6,10},{7,11},{8,12},{9,13},{1... | collective-permute-start | bytes 2064392 | tf_op jit(solution)/shard_map/ppermute | solution.py:37
  25.7 10.1 %collective-permute-start.3 = (bf16[64,3584]{1,0:T(8,128)(2,1)S(1)}, bf16[64,3584]{1,0:T(8,128)(2,1)S(1)}, u32[]{:S(2)}, u32[]{:S(2)}) collective-permute-start(bf16[64,3584]{1,0:T(8,128)(2,1)S(1)} %norm.1.after.n0), channel_id=1, source_target_pairs={{0,3},{1,0},{2,1},{3,2},{4,7},{5,4},{6,5},{7,6},{8,11},{9,8},{10,9... | collective-permute-start | bytes 1376264 | tf_op jit(solution)/shard_map/ppermute | solution.py:37
  25.7 10.1 %collective-permute-start.4 = (bf16[64,3584]{1,0:T(8,128)(2,1)S(1)}, bf16[64,3584]{1,0:T(8,128)(2,1)S(1)}, u32[]{:S(2)}, u32[]{:S(2)}) collective-permute-start(bf16[64,3584]{1,0:T(8,128)(2,1)S(1)} %norm.1.after.n0), channel_id=1, source_target_pairs={{0,1},{1,2},{2,3},{3,0},{4,5},{5,6},{6,7},{7,4},{8,9},{9,10},{10,1... | collective-permute-start | bytes 1376264 | tf_op jit(solution)/shard_map/ppermute | solution.py:37
  38.1 11.9 %collective-permute-start.14 = (bf16[12,112,768]{2,1,0:T(8,128)(2,1)S(1)}, bf16[12,112,768]{2,1,0:T(8,128)(2,1)S(1)}, u32[]{:S(2)}, u32[]{:S(2)}) collective-permute-start(bf16[12,112,768]{2,1,0:T(8,128)(2,1)S(1)} %get-tuple-element.32.own1), channel_id=1, source_target_pairs={{0,16},{1,17},{2,18},{3,19},{4,20},{5,21},{6,22},{7,23},{8,24},{9,... | collective-permute-start | bytes 6193160 | tf_op jit(solution)/shard_map/ppermute | solution.py:37
  38.2 11.6 %collective-permute-start.12 = (bf16[2,112,768]{2,1,0:T(8,128)(2,1)S(1)}, bf16[2,112,768]{2,1,0:T(8,128)(2,1)S(1)}, u32[]{:S(2)}, u32[]{:S(2)}) collective-permute-start(bf16[2,112,768]{2,1,0:T(8,128)(2,1)S(1)} %get-tuple-element.35), channel_id=1, source_target_pairs={{0,12},{1,13},{2,14},{3,15},{4,0},{5,1},{6,2},{7,3},{8,4},{9,5},{1... | collective-permute-start | bytes 1032200 | tf_op jit(solution)/shard_map/ppermute | solution.py:37
  39.2 10.6 %collective-permute-start.13 = (bf16[2,112,768]{2,1,0:T(8,128)(2,1)S(1)}, bf16[2,112,768]{2,1,0:T(8,128)(2,1)S(1)}, u32[]{:S(2)}, u32[]{:S(2)}) collective-permute-start(bf16[2,112,768]{2,1,0:T(8,128)(2,1)S(1)} %get-tuple-element.36), channel_id=1, source_target_pairs={{0,4},{1,5},{2,6},{3,7},{4,8},{5,9},{6,10},{7,11},{8,12},{9,13},{1... | collective-permute-start | bytes 1032200 | tf_op jit(solution)/shard_map/ppermute | solution.py:37
  40.3 9.5 %collective-permute-start.10 = (bf16[32,3584]{1,0:T(8,128)(2,1)S(1)}, bf16[32,3584]{1,0:T(8,128)(2,1)S(1)}, u32[]{:S(2)}, u32[]{:S(2)}) collective-permute-start(bf16[32,3584]{1,0:T(8,128)(2,1)S(1)} %get-tuple-element.33), channel_id=1, source_target_pairs={{0,3},{1,0},{2,1},{3,2},{4,7},{5,4},{6,5},{7,6},{8,11},{9,8},{10,9... | collective-permute-start | bytes 688136 | tf_op jit(solution)/shard_map/ppermute | solution.py:37
  40.3 9.5 %collective-permute-start.11 = (bf16[32,3584]{1,0:T(8,128)(2,1)S(1)}, bf16[32,3584]{1,0:T(8,128)(2,1)S(1)}, u32[]{:S(2)}, u32[]{:S(2)}) collective-permute-start(bf16[32,3584]{1,0:T(8,128)(2,1)S(1)} %get-tuple-element.34), channel_id=1, source_target_pairs={{0,1},{1,2},{2,3},{3,0},{4,5},{5,6},{6,7},{7,4},{8,9},{9,10},{10,1... | collective-permute-start | bytes 688136 | tf_op jit(solution)/shard_map/ppermute | solution.py:37
  52.9 9.6 %collective-permute-start.17 = (bf16[256,256]{1,0:T(8,128)(2,1)S(1)}, bf16[256,256]{1,0:T(8,128)(2,1)S(1)}, u32[]{:S(2)}, u32[]{:S(2)}) collective-permute-start(bf16[256,256]{1,0:T(8,128)(2,1)S(1)} %get-tuple-element.41.a0), channel_id=1, source_target_pairs={{0,4},{1,5},{2,6},{3,7},{4,8},{5,9},{6,10},{7,11},{8,12},{9,13},{1... | collective-permute-start | bytes 393224 | tf_op jit(solution)/shard_map/ppermute | solution.py:37
  52.9 10.9 %collective-permute-start.16 = (bf16[256,256]{1,0:T(8,128)(2,1)S(1)}, bf16[256,256]{1,0:T(8,128)(2,1)S(1)}, u32[]{:S(2)}, u32[]{:S(2)}) collective-permute-start(bf16[256,256]{1,0:T(8,128)(2,1)S(1)} %get-tuple-element.41.a0), channel_id=1, source_target_pairs={{0,8},{1,9},{2,10},{3,11},{4,12},{5,13},{6,14},{7,15},{8,0},{9,1},... | collective-permute-start | bytes 393224 | tf_op jit(solution)/shard_map/ppermute | solution.py:37
  55.6 8.3 %collective-permute-start.18 = (bf16[256,256]{1,0:T(8,128)(2,1)S(1)}, bf16[256,256]{1,0:T(8,128)(2,1)S(1)}, u32[]{:S(2)}, u32[]{:S(2)}) collective-permute-start(bf16[256,256]{1,0:T(8,128)(2,1)S(1)} %get-tuple-element.41.a0), channel_id=1, source_target_pairs={{0,12},{1,13},{2,14},{3,15},{4,0},{5,1},{6,2},{7,3},{8,4},{9,5},{1... | collective-permute-start | bytes 393224 | tf_op jit(solution)/shard_map/ppermute | solution.py:37
  56.2 7.7 %collective-permute-start.19 = (bf16[256,256]{1,0:T(8,128)(2,1)S(1)}, bf16[256,256]{1,0:T(8,128)(2,1)S(1)}, u32[]{:S(2)}, u32[]{:S(2)}) collective-permute-start(bf16[256,256]{1,0:T(8,128)(2,1)S(1)} %get-tuple-element.41.a0), channel_id=1, source_target_pairs={{0,1},{1,0},{2,3},{3,2},{4,5},{5,4},{6,7},{7,6},{8,9},{9,8},{10,11... | collective-permute-start | bytes 393224 | tf_op jit(solution)/shard_map/ppermute | solution.py:37
  62.5 15.3 %collective-permute-start.26 = (bf16[256,256]{1,0:T(8,128)(2,1)S(1)}, bf16[256,256]{1,0:T(8,128)(2,1)S(1)}, u32[]{:S(2)}, u32[]{:S(2)}) collective-permute-start(bf16[256,256]{1,0:T(8,128)(2,1)S(1)} %collective-permute-done.17.a3), channel_id=1, source_target_pairs={{0,1},{1,0},{2,3},{3,2},{4,5},{5,4},{6,7},{7,6},{8,9},{9,8},{10,11... | collective-permute-start | bytes 393224 | tf_op jit(solution)/shard_map/ppermute | solution.py:37
  64.1 6.7 %collective-permute-start.20 = (bf16[64,256]{1,0:T(8,128)(2,1)S(1)}, bf16[64,256]{1,0:T(8,128)(2,1)S(1)}, u32[]{:S(2)}, u32[]{:S(2)}) collective-permute-start(bf16[64,256]{1,0:T(8,128)(2,1)S(1)} %get-tuple-element.45), channel_id=1, source_target_pairs={{0,2},{1,3},{2,0},{3,1},{4,6},{5,7},{6,4},{7,5},{8,10},{9,11},{10,... | collective-permute-start | bytes 98312 | tf_op jit(solution)/shard_map/ppermute | solution.py:37
  68.6 4.1 %collective-permute-start.21 = (bf16[64,256]{1,0:T(8,128)(2,1)S(1)}, bf16[64,256]{1,0:T(8,128)(2,1)S(1)}, u32[]{:S(2)}, u32[]{:S(2)}) collective-permute-start(bf16[64,256]{1,0:T(8,128)(2,1)S(1)} %get-tuple-element.46), channel_id=1, source_target_pairs={{0,1},{1,2},{2,3},{3,0},{4,5},{5,6},{6,7},{7,4},{8,9},{9,10},{10,1... | collective-permute-start | bytes 98312 | tf_op jit(solution)/shard_map/ppermute | solution.py:37
  68.9 5.1 %collective-permute-start.22 = (bf16[64,256]{1,0:T(8,128)(2,1)S(1)}, bf16[64,256]{1,0:T(8,128)(2,1)S(1)}, u32[]{:S(2)}, u32[]{:S(2)}) collective-permute-start(bf16[64,256]{1,0:T(8,128)(2,1)S(1)} %get-tuple-element.47), channel_id=1, source_target_pairs={{0,3},{1,0},{2,1},{3,2},{4,7},{5,4},{6,5},{7,6},{8,11},{9,8},{10,9... | collective-permute-start | bytes 98312 | tf_op jit(solution)/shard_map/ppermute | solution.py:37
  70.6 9.2 %collective-permute-start.27 = (bf16[256,256]{1,0:T(8,128)(2,1)S(1)}, bf16[256,256]{1,0:T(8,128)(2,1)S(1)}, u32[]{:S(2)}, u32[]{:S(2)}) collective-permute-start(bf16[256,256]{1,0:T(8,128)(2,1)S(1)} %collective-permute-done.16.a2), channel_id=1, source_target_pairs={{0,1},{1,0},{2,3},{3,2},{4,5},{5,4},{6,7},{7,6},{8,9},{9,8},{10,11... | collective-permute-start | bytes 393224 | tf_op jit(solution)/shard_map/ppermute | solution.py:37
  70.8 9.0 %collective-permute-start.28 = (bf16[256,256]{1,0:T(8,128)(2,1)S(1)}, bf16[256,256]{1,0:T(8,128)(2,1)S(1)}, u32[]{:S(2)}, u32[]{:S(2)}) collective-permute-start(bf16[256,256]{1,0:T(8,128)(2,1)S(1)} %collective-permute-done.18.a1), channel_id=1, source_target_pairs={{0,1},{1,0},{2,3},{3,2},{4,5},{5,4},{6,7},{7,6},{8,9},{9,8},{10,11... | collective-permute-start | bytes 393224 | tf_op jit(solution)/shard_map/ppermute | solution.py:37
  74.1 7.5 %collective-permute-start.23 = (bf16[64,768]{1,0:T(8,128)(2,1)S(1)}, bf16[64,768]{1,0:T(8,128)(2,1)S(1)}, u32[]{:S(2)}, u32[]{:S(2)}) collective-permute-start(bf16[64,768]{1,0:T(8,128)(2,1)S(1)} %cache_heads.1.after.c0), channel_id=1, source_target_pairs={{0,64},{1,65},{2,66},{3,67},{4,68},{5,69},{6,70},{7,71},{8,72},{9,... | collective-permute-start | bytes 294920 | tf_op jit(solution)/shard_map/ppermute | solution.py:37
  75.3 6.3 %collective-permute-start.24 = (bf16[64,768]{1,0:T(8,128)(2,1)S(1)}, bf16[64,768]{1,0:T(8,128)(2,1)S(1)}, u32[]{:S(2)}, u32[]{:S(2)}) collective-permute-start(bf16[64,768]{1,0:T(8,128)(2,1)S(1)} %cache_heads.1.after.c0), channel_id=1, source_target_pairs={{0,32},{1,33},{2,34},{3,35},{4,36},{5,37},{6,38},{7,39},{8,40},{9,... | collective-permute-start | bytes 294920 | tf_op jit(solution)/shard_map/ppermute | solution.py:37
  77.8 4.6 %collective-permute-start.25 = (bf16[64,768]{1,0:T(8,128)(2,1)S(1)}, bf16[64,768]{1,0:T(8,128)(2,1)S(1)}, u32[]{:S(2)}, u32[]{:S(2)}) collective-permute-start(bf16[64,768]{1,0:T(8,128)(2,1)S(1)} %cache_heads.1.after.c0), channel_id=1, source_target_pairs={{0,96},{1,97},{2,98},{3,99},{4,100},{5,101},{6,102},{7,103},{8,104... | collective-permute-start | bytes 294920 | tf_op jit(solution)/shard_map/ppermute | solution.py:37
  82.4 9.1 %collective-permute-start.29 = (bf16[4,64,768]{2,1,0:T(8,128)(2,1)S(1)}, bf16[4,64,768]{2,1,0:T(8,128)(2,1)S(1)}, u32[]{:S(2)}, u32[]{:S(2)}) collective-permute-start(bf16[4,64,768]{2,1,0:T(8,128)(2,1)S(1)} %cache_join.1.own), channel_id=1, source_target_pairs={{0,16},{1,17},{2,18},{3,19},{4,20},{5,21},{6,22},{7,23},{8,24},{9,... | collective-permute-start | bytes 1179656 | tf_op jit(solution)/shard_map/ppermute | solution.py:37
  82.5 6.0 %collective-permute-start.30 = (bf16[64,512]{1,0:T(8,128)(2,1)S(1)}, bf16[64,512]{1,0:T(8,128)(2,1)S(1)}, u32[]{:S(2)}, u32[]{:S(2)}) collective-permute-start(bf16[64,512]{1,0:T(8,128)(2,1)S(1)} %get-tuple-element.51), channel_id=1, source_target_pairs={{0,2},{1,3},{2,0},{3,1},{4,6},{5,7},{6,4},{7,5},{8,10},{9,11},{10,... | collective-permute-start | bytes 196616 | tf_op jit(solution)/shard_map/ppermute | solution.py:37
  83.5 5.1 %collective-permute-start.31 = (bf16[64,512]{1,0:T(8,128)(2,1)S(1)}, bf16[64,512]{1,0:T(8,128)(2,1)S(1)}, u32[]{:S(2)}, u32[]{:S(2)}) collective-permute-start(bf16[64,512]{1,0:T(8,128)(2,1)S(1)} %get-tuple-element.52), channel_id=1, source_target_pairs={{0,1},{1,2},{2,3},{3,0},{4,5},{5,6},{6,7},{7,4},{8,9},{9,10},{10,1... | collective-permute-start | bytes 196616 | tf_op jit(solution)/shard_map/ppermute | solution.py:37
  86.0 5.5 %collective-permute-start.32 = (bf16[64,512]{1,0:T(8,128)(2,1)S(1)}, bf16[64,512]{1,0:T(8,128)(2,1)S(1)}, u32[]{:S(2)}, u32[]{:S(2)}) collective-permute-start(bf16[64,512]{1,0:T(8,128)(2,1)S(1)} %get-tuple-element.53), channel_id=1, source_target_pairs={{0,3},{1,0},{2,1},{3,2},{4,7},{5,4},{6,5},{7,6},{8,11},{9,8},{10,9... | collective-permute-start | bytes 196616 | tf_op jit(solution)/shard_map/ppermute | solution.py:37
  (9 other events, 131.9 us)

commit v2 on v0

--- a/solution.py
+++ b/solution.py
@@ -301,8 +301,8 @@
         out[:, (3 + k) * HEAD : (4 + k) * HEAD] = buf[src, :, HEAD:]
 
 
-def cache_join(c0, c2, c1, c3, after, out):
-    for n, c in zip(HOPS, (c0, c2, c1, c3)):
+def cache_join(c0, c2, c3, c1, after, out):
+    for n, c in enumerate((c0, c1, c2, c3)):
         out[n] = c[...]
 
 
@@ -414,7 +414,7 @@
     (cached,) = call(
         cache_join,
         [((4, 64, 768), bf)],
-        (mine, *spread(lambda j: send(mine, along_z(-j))), outs[0]),
+        (mine, *[send(mine, along_z(-j)) for j in (2, 3, 1)], outs[0]),
         [VM] * 4 + [ANY],
     )
     attended, cache = call(

time: 91.8 us -> 91.4 us (level)
  waiting for transfers between devices: 36.7 us -> 35.4 us
    ppermute x33, waiting for transfers between devices: 36.7 us -> 35.4 us  [send(): return lax.ppermute(v, EVERY, [(flat(*p), flat(*move(*p))) for p in PLACES])]
    ppermute x33, starting transfers between devices: 40.7 us -> 41.6 us  [send(): return lax.ppermute(v, EVERY, [(flat(*p), flat(*move(*p))) for p in PLACES])]
  transfers between devices with their start and end apart: 33 -> 33, of which waited for: 16 -> 15; matrix products, arithmetic and copies ran while one was open for 0% -> 0% of each run, Pallas kernels for 7% -> 7%
where the time goes in v2:
time: 91.4 us; the launch traced here: 91.1 us
  starting transfers between devices  41.6 us (46%)
  waiting for transfers between devices  35.4 us (39%)
  Pallas kernels  10.7 us (12%)
  local copies, waits for them, and re-layouts  2.57 us (3%)
    ppermute x33, starting transfers between devices, send(): return lax.ppermute(v, EVERY, [(flat(*p), flat(*move(*p))) for p in PLACES])  41.6 us
    ppermute x33, waiting for transfers between devices, send(): return lax.ppermute(v, EVERY, [(flat(*p), flat(*move(*p))) for p in PLACES])  35.4 us
    pallas_call x16, Pallas kernels, call(): pl.pallas_call(kernel, out_shape=outs, in_specs=[VM] * len(operands) if i...  10.7 us
    unnamed x16, local copies, waits for them, and re-layouts  2.57 us
  transfers between devices with their start and end apart: 33, of which 15 were waited for; matrix products, arithmetic and copies ran while one was open for 0% of the time, Pallas kernels for 7%

profile of v2, /device:TPU:6, one launch (start us, length us, event | category | flops | bytes accessed | tf_op | source)
XLA Modules:
  0.0 91.1 jit_solution(3784438385938277893)
XLA Ops:
  0.6 1.6 %cut.1 = (bf16[28,768]{1,0:T(8,128)(2,1)}, bf16[28,768]{1,0:T(8,128)(2,1)}, bf16[28,768]{1,0:T(8,128)(2,1)}, bf16[28,768]{1,0:T(8,128)(2,1)}) custom-call(bf16[28,2048]{1,0:T(8,128)(2,1)} %wq.1, bf16[28,768]{1,0:T(8,128)(2,1)} %wkv.1), custom_call_target="tpu_custom_call" | custom-call | tf_op jit(solution)/shard_map/cut/pallas_call | solution.py:77
  2.2 1.5 %collective-permute-start = (bf16[28,768]{1,0:T(8,128)(2,1)}, bf16[28,768]{1,0:T(8,128)(2,1)S(1)}, u32[]{:S(2)}, u32[]{:S(2)}) collective-permute-start(bf16[28,768]{1,0:T(8,128)(2,1)} %get-tuple-element.29), channel_id=1, source_target_pairs={{0,2},{1,3},{2,0},{3,1},{4,6},{5,7},{6,4},{7,5},{8,10},{9,11},{10,... | collective-permute-start | bytes 129032 | tf_op jit(solution)/shard_map/ppermute | solution.py:37
  3.7 2.1 %collective-permute-start.1 = (bf16[28,768]{1,0:T(8,128)(2,1)}, bf16[28,768]{1,0:T(8,128)(2,1)S(1)}, u32[]{:S(2)}, u32[]{:S(2)}) collective-permute-start(bf16[28,768]{1,0:T(8,128)(2,1)} %get-tuple-element.30), channel_id=1, source_target_pairs={{0,1},{1,2},{2,3},{3,0},{4,5},{5,6},{6,7},{7,4},{8,9},{9,10},{10,1... | collective-permute-start | bytes 129032 | tf_op jit(solution)/shard_map/ppermute | solution.py:37
  6.7 1.6 %collective-permute-done.p2 = bf16[28,768]{1,0:T(8,128)(2,1)S(1)} collective-permute-done((bf16[28,768]{1,0:T(8,128)(2,1)}, bf16[28,768]{1,0:T(8,128)(2,1)S(1)}, u32[]{:S(2)}, u32[]{:S(2)}) %collective-permute-start) | collective-permute-done | bytes 43040 | tf_op jit(solution)/shard_map/ppermute | solution.py:37
  8.3 3.0 %collective-permute-done.2.p3 = bf16[28,768]{1,0:T(8,128)(2,1)S(1)} collective-permute-done((bf16[28,768]{1,0:T(8,128)(2,1)}, bf16[28,768]{1,0:T(8,128)(2,1)S(1)}, u32[]{:S(2)}, u32[]{:S(2)}) %collective-permute-start.2) | collective-permute-done | bytes 43040 | tf_op jit(solution)/shard_map/ppermute | solution.py:37
  11.4 4.0 %collective-permute-start.5 = (bf16[112,768]{1,0:T(8,128)(2,1)S(1)}, bf16[112,768]{1,0:T(8,128)(2,1)S(1)}, u32[]{:S(2)}, u32[]{:S(2)}) collective-permute-start(bf16[112,768]{1,0:T(8,128)(2,1)S(1)} %place.1.after.s0), channel_id=1, source_target_pairs={{0,64},{1,65},{2,66},{3,67},{4,68},{5,69},{6,70},{7,71},{8,72},{9,... | collective-permute-start | bytes 516104 | tf_op jit(solution)/shard_map/ppermute | solution.py:37
  16.1 1.3 %collective-permute-start.7 = (bf16[112,768]{1,0:T(8,128)(2,1)S(1)}, bf16[112,768]{1,0:T(8,128)(2,1)S(1)}, u32[]{:S(2)}, u32[]{:S(2)}) collective-permute-start(bf16[112,768]{1,0:T(8,128)(2,1)S(1)} %place.1.after.s0), channel_id=1, source_target_pairs={{0,32},{1,33},{2,34},{3,35},{4,36},{5,37},{6,38},{7,39},{8,40},{9,... | collective-permute-start | bytes 516104 | tf_op jit(solution)/shard_map/ppermute | solution.py:37
  19.3 2.3 %collective-permute-done.6.s1 = bf16[112,768]{1,0:T(8,128)(2,1)S(1)} collective-permute-done((bf16[112,768]{1,0:T(8,128)(2,1)S(1)}, bf16[112,768]{1,0:T(8,128)(2,1)S(1)}, u32[]{:S(2)}, u32[]{:S(2)}) %collective-permute-start.6) | collective-permute-done | bytes 172064 | tf_op jit(solution)/shard_map/ppermute | solution.py:37
  22.8 3.3 %collective-permute-start.8 = (bf16[4,112,768]{2,1,0:T(8,128)(2,1)S(1)}, bf16[4,112,768]{2,1,0:T(8,128)(2,1)S(1)}, u32[]{:S(2)}, u32[]{:S(2)}) collective-permute-start(bf16[4,112,768]{2,1,0:T(8,128)(2,1)S(1)} %stage.1.s0), channel_id=1, source_target_pairs={{0,12},{1,13},{2,14},{3,15},{4,0},{5,1},{6,2},{7,3},{8,4},{9,5},{1... | collective-permute-start | bytes 2064392 | tf_op jit(solution)/shard_map/ppermute | solution.py:37
  26.1 3.2 %collective-permute-start.4 = (bf16[64,3584]{1,0:T(8,128)(2,1)S(1)}, bf16[64,3584]{1,0:T(8,128)(2,1)S(1)}, u32[]{:S(2)}, u32[]{:S(2)}) collective-permute-start(bf16[64,3584]{1,0:T(8,128)(2,1)S(1)} %norm.1.after.n0), channel_id=1, source_target_pairs={{0,1},{1,2},{2,3},{3,0},{4,5},{5,6},{6,7},{7,4},{8,9},{9,10},{10,1... | collective-permute-start | bytes 1376264 | tf_op jit(solution)/shard_map/ppermute | solution.py:37
  29.3 7.3 %collective-permute-done.3.n1 = bf16[64,3584]{1,0:T(8,128)(2,1)S(1)} collective-permute-done((bf16[64,3584]{1,0:T(8,128)(2,1)S(1)}, bf16[64,3584]{1,0:T(8,128)(2,1)S(1)}, u32[]{:S(2)}, u32[]{:S(2)}) %collective-permute-start.3) | collective-permute-done | bytes 458784 | tf_op jit(solution)/shard_map/ppermute | solution.py:37
  36.6 1.6 %collective-permute-done.9.s3 = bf16[4,112,768]{2,1,0:T(8,128)(2,1)S(1)} collective-permute-done((bf16[4,112,768]{2,1,0:T(8,128)(2,1)S(1)}, bf16[4,112,768]{2,1,0:T(8,128)(2,1)S(1)}, u32[]{:S(2)}, u32[]{:S(2)}) %collective-permute-start.9) | collective-permute-done | bytes 688160 | tf_op jit(solution)/shard_map/ppermute | solution.py:37
  39.4 1.2 %collective-permute-start.13 = (bf16[2,112,768]{2,1,0:T(8,128)(2,1)S(1)}, bf16[2,112,768]{2,1,0:T(8,128)(2,1)S(1)}, u32[]{:S(2)}, u32[]{:S(2)}) collective-permute-start(bf16[2,112,768]{2,1,0:T(8,128)(2,1)S(1)} %get-tuple-element.36), channel_id=1, source_target_pairs={{0,4},{1,5},{2,6},{3,7},{4,8},{5,9},{6,10},{7,11},{8,12},{9,13},{1... | collective-permute-start | bytes 1032200 | tf_op jit(solution)/shard_map/ppermute | solution.py:37
  40.6 3.2 %collective-permute-start.11 = (bf16[32,3584]{1,0:T(8,128)(2,1)S(1)}, bf16[32,3584]{1,0:T(8,128)(2,1)S(1)}, u32[]{:S(2)}, u32[]{:S(2)}) collective-permute-start(bf16[32,3584]{1,0:T(8,128)(2,1)S(1)} %get-tuple-element.34), channel_id=1, source_target_pairs={{0,1},{1,2},{2,3},{3,0},{4,5},{5,6},{6,7},{7,4},{8,9},{9,10},{10,1... | collective-permute-start | bytes 688136 | tf_op jit(solution)/shard_map/ppermute | solution.py:37
  43.8 5.3 %collective-permute-done.10.after1.n2a = bf16[32,3584]{1,0:T(8,128)(2,1)S(1)} collective-permute-done((bf16[32,3584]{1,0:T(8,128)(2,1)S(1)}, bf16[32,3584]{1,0:T(8,128)(2,1)S(1)}, u32[]{:S(2)}, u32[]{:S(2)}) %collective-permute-start.10) | collective-permute-done | bytes 229408 | tf_op jit(solution)/shard_map/ppermute | solution.py:37
  49.4 1.4 %gather.1 = (bf16[32,112,768]{2,1,0:T(8,128)(2,1)S(1)}, bf16[256,3584]{1,0:T(8,128)(2,1)S(1)}, f32[256,128]{1,0:T(8,128)S(1)}, f32[512]{0:T(512)S(1)}, f32[2,128]{1,0:T(2,128)S(1)}) custom-call(s32[8,16]{1,0:T(8,128)S(1)} %copy-done.3, bf16[12,112,768]{2,1,0:T(8,128)(2,1)S(1)} %get-tuple-element.32.own1, bf16[4,112,768]{2,1,0:T(8,128)(2,1)S(1)} %join2.1.own2, ...), custom_call_target="tpu_custom_call" | custom-call | tf_op jit(solution)/shard_map/gather/pallas_call | solution.py:77
  56.2 2.5 %collective-permute-done.17.a1 = bf16[256,256]{1,0:T(8,128)(2,1)S(1)} collective-permute-done((bf16[256,256]{1,0:T(8,128)(2,1)S(1)}, bf16[256,256]{1,0:T(8,128)(2,1)S(1)}, u32[]{:S(2)}, u32[]{:S(2)}) %collective-permute-start.17) | collective-permute-done | bytes 131104 | tf_op jit(solution)/shard_map/ppermute | solution.py:37
  59.5 1.4 %q_project.1.after1.q = bf16[256,512]{1,0:T(8,128)(2,1)S(1)} custom-call(bf16[32,112,768]{2,1,0:T(8,128)(2,1)S(1)} %get-tuple-element.42.w, bf16[256,3584]{1,0:T(8,128)(2,1)S(1)} %get-tuple-element.38.x_in, f32[256,128]{1,0:T(8,128)S(1)} %get-tuple-element.39.cs, f32[512]{0:T(512)S(1)} %get-tuple-element.43.qb), custom_call_target="tpu_custom_call" | custom-call | tf_op jit(solution)/shard_map/q_project/pallas_call | solution.py:77
  61.3 1.7 %collective-permute-done.18.a3 = bf16[256,256]{1,0:T(8,128)(2,1)S(1)} collective-permute-done((bf16[256,256]{1,0:T(8,128)(2,1)S(1)}, bf16[256,256]{1,0:T(8,128)(2,1)S(1)}, u32[]{:S(2)}, u32[]{:S(2)}) %collective-permute-start.18) | collective-permute-done | bytes 131104 | tf_op jit(solution)/shard_map/ppermute | solution.py:37
  63.2 3.1 %collective-permute-start.20 = (bf16[64,256]{1,0:T(8,128)(2,1)S(1)}, bf16[64,256]{1,0:T(8,128)(2,1)S(1)}, u32[]{:S(2)}, u32[]{:S(2)}) collective-permute-start(bf16[64,256]{1,0:T(8,128)(2,1)S(1)} %get-tuple-element.45), channel_id=1, source_target_pairs={{0,2},{1,3},{2,0},{3,1},{4,6},{5,7},{6,4},{7,5},{8,10},{9,11},{10,... | collective-permute-start | bytes 98312 | tf_op jit(solution)/shard_map/ppermute | solution.py:37
  67.1 1.3 %collective-permute-start.22 = (bf16[64,256]{1,0:T(8,128)(2,1)S(1)}, bf16[64,256]{1,0:T(8,128)(2,1)S(1)}, u32[]{:S(2)}, u32[]{:S(2)}) collective-permute-start(bf16[64,256]{1,0:T(8,128)(2,1)S(1)} %get-tuple-element.47), channel_id=1, source_target_pairs={{0,3},{1,0},{2,1},{3,2},{4,7},{5,4},{6,5},{7,6},{8,11},{9,8},{10,9... | collective-permute-start | bytes 98312 | tf_op jit(solution)/shard_map/ppermute | solution.py:37
  69.2 1.2 %collective-permute-start.28 = (bf16[256,256]{1,0:T(8,128)(2,1)S(1)}, bf16[256,256]{1,0:T(8,128)(2,1)S(1)}, u32[]{:S(2)}, u32[]{:S(2)}) collective-permute-start(bf16[256,256]{1,0:T(8,128)(2,1)S(1)} %collective-permute-done.18.a3), channel_id=1, source_target_pairs={{0,1},{1,0},{2,3},{3,2},{4,5},{5,4},{6,7},{7,6},{8,9},{9,8},{10,11... | collective-permute-start | bytes 393224 | tf_op jit(solution)/shard_map/ppermute | solution.py:37
  70.4 1.8 %collective-permute-done.22.t3 = bf16[64,256]{1,0:T(8,128)(2,1)S(1)} collective-permute-done((bf16[64,256]{1,0:T(8,128)(2,1)S(1)}, bf16[64,256]{1,0:T(8,128)(2,1)S(1)}, u32[]{:S(2)}, u32[]{:S(2)}) %collective-permute-start.22) | collective-permute-done | bytes 32800 | tf_op jit(solution)/shard_map/ppermute | solution.py:37
  72.3 1.6 %collective-permute-start.23 = (bf16[64,768]{1,0:T(8,128)(2,1)S(1)}, bf16[64,768]{1,0:T(8,128)(2,1)S(1)}, u32[]{:S(2)}, u32[]{:S(2)}) collective-permute-start(bf16[64,768]{1,0:T(8,128)(2,1)S(1)} %cache_heads.1.after.c0), channel_id=1, source_target_pairs={{0,64},{1,65},{2,66},{3,67},{4,68},{5,69},{6,70},{7,71},{8,72},{9,... | collective-permute-start | bytes 294920 | tf_op jit(solution)/shard_map/ppermute | solution.py:37
  73.8 2.3 %collective-permute-start.24 = (bf16[64,768]{1,0:T(8,128)(2,1)S(1)}, bf16[64,768]{1,0:T(8,128)(2,1)S(1)}, u32[]{:S(2)}, u32[]{:S(2)}) collective-permute-start(bf16[64,768]{1,0:T(8,128)(2,1)S(1)} %cache_heads.1.after.c0), channel_id=1, source_target_pairs={{0,32},{1,33},{2,34},{3,35},{4,36},{5,37},{6,38},{7,39},{8,40},{9,... | collective-permute-start | bytes 294920 | tf_op jit(solution)/shard_map/ppermute | solution.py:37
  77.1 1.2 %attend_own.1 = (f32[256,1024]{1,0:T(8,128)S(1)}, bf16[256,128]{1,0:T(8,128)(2,1)S(1)}) custom-call(s32[8,16]{1,0:T(8,128)S(1)} %copy-done.3, bf16[256,512]{1,0:T(8,128)(2,1)S(1)} %q_project.1.after1.q, bf16[256,256]{1,0:T(8,128)(2,1)S(1)} %get-tuple-element.41.a0, bf16[256,256]{1,0:T(8,128)(2,1)S(1)} %collective-permute-done.17.a1, ...), custom_call_target="tpu_custom_call" | custom-call | tf_op jit(solution)/shard_map/attend_own/pallas_call | solution.py:77
  78.4 1.7 %attend.1 = (bf16[64,512]{1,0:T(8,128)(2,1)S(1)}, bf16[64,512]{1,0:T(8,128)(2,1)S(1)}, bf16[64,512]{1,0:T(8,128)(2,1)S(1)}, bf16[64,512]{1,0:T(8,128)(2,1)S(1)}) custom-call(f32[256,1024]{1,0:T(8,128)S(1)} %get-tuple-element.48.mask, bf16[256,128]{1,0:T(8,128)(2,1)S(1)} %get-tuple-element.49.last, bf16[256,512]{1,0:T(8,128)(2,1)S(1)} %q_project.1.after1.q, ...), custom_call_target="tpu_custom_call" | custom-call | tf_op jit(solution)/shard_map/attend/pallas_call | solution.py:77
  80.9 1.3 %collective-permute-start.30 = (bf16[64,512]{1,0:T(8,128)(2,1)S(1)}, bf16[64,512]{1,0:T(8,128)(2,1)S(1)}, u32[]{:S(2)}, u32[]{:S(2)}) collective-permute-start(bf16[64,512]{1,0:T(8,128)(2,1)S(1)} %get-tuple-element.51), channel_id=1, source_target_pairs={{0,2},{1,3},{2,0},{3,1},{4,6},{5,7},{6,4},{7,5},{8,10},{9,11},{10,... | collective-permute-start | bytes 196616 | tf_op jit(solution)/shard_map/ppermute | solution.py:37
  82.2 1.8 %collective-permute-start.31 = (bf16[64,512]{1,0:T(8,128)(2,1)S(1)}, bf16[64,512]{1,0:T(8,128)(2,1)S(1)}, u32[]{:S(2)}, u32[]{:S(2)}) collective-permute-start(bf16[64,512]{1,0:T(8,128)(2,1)S(1)} %get-tuple-element.52), channel_id=1, source_target_pairs={{0,1},{1,2},{2,3},{3,0},{4,5},{5,6},{6,7},{7,4},{8,9},{9,10},{10,1... | collective-permute-start | bytes 196616 | tf_op jit(solution)/shard_map/ppermute | solution.py:37
  84.2 2.7 %collective-permute-done.30.r2 = bf16[64,512]{1,0:T(8,128)(2,1)S(1)} collective-permute-done((bf16[64,512]{1,0:T(8,128)(2,1)S(1)}, bf16[64,512]{1,0:T(8,128)(2,1)S(1)}, u32[]{:S(2)}, u32[]{:S(2)}) %collective-permute-start.30) | collective-permute-done | bytes 65568 | tf_op jit(solution)/shard_map/ppermute | solution.py:37
  86.9 2.5 %collective-permute-done.32.r3 = bf16[64,512]{1,0:T(8,128)(2,1)S(1)} collective-permute-done((bf16[64,512]{1,0:T(8,128)(2,1)S(1)}, bf16[64,512]{1,0:T(8,128)(2,1)S(1)}, u32[]{:S(2)}, u32[]{:S(2)}) %collective-permute-start.32) | collective-permute-done | bytes 65568 | tf_op jit(solution)/shard_map/ppermute | solution.py:37
  89.4 1.7 %finish.1 = (bf16[64,2048]{1,0:T(8,128)(2,1)}, bf16[1,1,512,768]{3,2,1,0:T(8,128)(2,1)}) custom-call(s32[8,16]{1,0:T(8,128)S(1)} %copy-done.7, bf16[4,64,768]{2,1,0:T(8,128)(2,1)S(1)} %cache_join.1.own, bf16[4,64,768]{2,1,0:T(8,128)(2,1)S(1)} %collective-permute-done.29.other, bf16[64,512]{1,0:T(8,128)(2,1)S(1)} %get-tuple-element.50.after.r0, ...), custom_call_target="tpu_custom_call" | custom-call | tf_op jit(solution)/shard_map/finish/pallas_call | solution.py:77
  (66 shorter events, 16.5 us)
Async XLA Ops:
  2.2 6.1 %collective-permute-start = (bf16[28,768]{1,0:T(8,128)(2,1)}, bf16[28,768]{1,0:T(8,128)(2,1)S(1)}, u32[]{:S(2)}, u32[]{:S(2)}) collective-permute-start(bf16[28,768]{1,0:T(8,128)(2,1)} %get-tuple-element.29), channel_id=1, source_target_pairs={{0,2},{1,3},{2,0},{3,1},{4,6},{5,7},{6,4},{7,5},{8,10},{9,11},{10,... | collective-permute-start | bytes 129032 | tf_op jit(solution)/shard_map/ppermute | solution.py:37
  3.7 4.6 %collective-permute-start.1 = (bf16[28,768]{1,0:T(8,128)(2,1)}, bf16[28,768]{1,0:T(8,128)(2,1)S(1)}, u32[]{:S(2)}, u32[]{:S(2)}) collective-permute-start(bf16[28,768]{1,0:T(8,128)(2,1)} %get-tuple-element.30), channel_id=1, source_target_pairs={{0,1},{1,2},{2,3},{3,0},{4,5},{5,6},{6,7},{7,4},{8,9},{9,10},{10,1... | collective-permute-start | bytes 129032 | tf_op jit(solution)/shard_map/ppermute | solution.py:37
  5.8 5.5 %collective-permute-start.2 = (bf16[28,768]{1,0:T(8,128)(2,1)}, bf16[28,768]{1,0:T(8,128)(2,1)S(1)}, u32[]{:S(2)}, u32[]{:S(2)}) collective-permute-start(bf16[28,768]{1,0:T(8,128)(2,1)} %get-tuple-element.31), channel_id=1, source_target_pairs={{0,3},{1,0},{2,1},{3,2},{4,7},{5,4},{6,5},{7,6},{8,11},{9,8},{10,9... | collective-permute-start | bytes 129032 | tf_op jit(solution)/shard_map/ppermute | solution.py:37
  11.4 7.9 %collective-permute-start.5 = (bf16[112,768]{1,0:T(8,128)(2,1)S(1)}, bf16[112,768]{1,0:T(8,128)(2,1)S(1)}, u32[]{:S(2)}, u32[]{:S(2)}) collective-permute-start(bf16[112,768]{1,0:T(8,128)(2,1)S(1)} %place.1.after.s0), channel_id=1, source_target_pairs={{0,64},{1,65},{2,66},{3,67},{4,68},{5,69},{6,70},{7,71},{8,72},{9,... | collective-permute-start | bytes 516104 | tf_op jit(solution)/shard_map/ppermute | solution.py:37
  15.4 6.3 %collective-permute-start.6 = (bf16[112,768]{1,0:T(8,128)(2,1)S(1)}, bf16[112,768]{1,0:T(8,128)(2,1)S(1)}, u32[]{:S(2)}, u32[]{:S(2)}) collective-permute-start(bf16[112,768]{1,0:T(8,128)(2,1)S(1)} %place.1.after.s0), channel_id=1, source_target_pairs={{0,96},{1,97},{2,98},{3,99},{4,100},{5,101},{6,102},{7,103},{8,104... | collective-permute-start | bytes 516104 | tf_op jit(solution)/shard_map/ppermute | solution.py:37
  16.1 6.6 %collective-permute-start.7 = (bf16[112,768]{1,0:T(8,128)(2,1)S(1)}, bf16[112,768]{1,0:T(8,128)(2,1)S(1)}, u32[]{:S(2)}, u32[]{:S(2)}) collective-permute-start(bf16[112,768]{1,0:T(8,128)(2,1)S(1)} %place.1.after.s0), channel_id=1, source_target_pairs={{0,32},{1,33},{2,34},{3,35},{4,36},{5,37},{6,38},{7,39},{8,40},{9,... | collective-permute-start | bytes 516104 | tf_op jit(solution)/shard_map/ppermute | solution.py:37
  22.8 13.8 %collective-permute-start.8 = (bf16[4,112,768]{2,1,0:T(8,128)(2,1)S(1)}, bf16[4,112,768]{2,1,0:T(8,128)(2,1)S(1)}, u32[]{:S(2)}, u32[]{:S(2)}) collective-permute-start(bf16[4,112,768]{2,1,0:T(8,128)(2,1)S(1)} %stage.1.s0), channel_id=1, source_target_pairs={{0,12},{1,13},{2,14},{3,15},{4,0},{5,1},{6,2},{7,3},{8,4},{9,5},{1... | collective-permute-start | bytes 2064392 | tf_op jit(solution)/shard_map/ppermute | solution.py:37
  26.0 12.1 %collective-permute-start.9 = (bf16[4,112,768]{2,1,0:T(8,128)(2,1)S(1)}, bf16[4,112,768]{2,1,0:T(8,128)(2,1)S(1)}, u32[]{:S(2)}, u32[]{:S(2)}) collective-permute-start(bf16[4,112,768]{2,1,0:T(8,128)(2,1)S(1)} %stage.1.s0), channel_id=1, source_target_pairs={{0,4},{1,5},{2,6},{3,7},{4,8},{5,9},{6,10},{7,11},{8,12},{9,13},{1... | collective-permute-start | bytes 2064392 | tf_op jit(solution)/shard_map/ppermute | solution.py:37
  26.1 10.6 %collective-permute-start.3 = (bf16[64,3584]{1,0:T(8,128)(2,1)S(1)}, bf16[64,3584]{1,0:T(8,128)(2,1)S(1)}, u32[]{:S(2)}, u32[]{:S(2)}) collective-permute-start(bf16[64,3584]{1,0:T(8,128)(2,1)S(1)} %norm.1.after.n0), channel_id=1, source_target_pairs={{0,3},{1,0},{2,1},{3,2},{4,7},{5,4},{6,5},{7,6},{8,11},{9,8},{10,9... | collective-permute-start | bytes 1376264 | tf_op jit(solution)/shard_map/ppermute | solution.py:37
  26.1 10.6 %collective-permute-start.4 = (bf16[64,3584]{1,0:T(8,128)(2,1)S(1)}, bf16[64,3584]{1,0:T(8,128)(2,1)S(1)}, u32[]{:S(2)}, u32[]{:S(2)}) collective-permute-start(bf16[64,3584]{1,0:T(8,128)(2,1)S(1)} %norm.1.after.n0), channel_id=1, source_target_pairs={{0,1},{1,2},{2,3},{3,0},{4,5},{5,6},{6,7},{7,4},{8,9},{9,10},{10,1... | collective-permute-start | bytes 1376264 | tf_op jit(solution)/shard_map/ppermute | solution.py:37
  38.4 10.9 %collective-permute-start.14 = (bf16[12,112,768]{2,1,0:T(8,128)(2,1)S(1)}, bf16[12,112,768]{2,1,0:T(8,128)(2,1)S(1)}, u32[]{:S(2)}, u32[]{:S(2)}) collective-permute-start(bf16[12,112,768]{2,1,0:T(8,128)(2,1)S(1)} %get-tuple-element.32.own1), channel_id=1, source_target_pairs={{0,16},{1,17},{2,18},{3,19},{4,20},{5,21},{6,22},{7,23},{8,24},{9,... | collective-permute-start | bytes 6193160 | tf_op jit(solution)/shard_map/ppermute | solution.py:37
  38.5 10.7 %collective-permute-start.12 = (bf16[2,112,768]{2,1,0:T(8,128)(2,1)S(1)}, bf16[2,112,768]{2,1,0:T(8,128)(2,1)S(1)}, u32[]{:S(2)}, u32[]{:S(2)}) collective-permute-start(bf16[2,112,768]{2,1,0:T(8,128)(2,1)S(1)} %get-tuple-element.35), channel_id=1, source_target_pairs={{0,12},{1,13},{2,14},{3,15},{4,0},{5,1},{6,2},{7,3},{8,4},{9,5},{1... | collective-permute-start | bytes 1032200 | tf_op jit(solution)/shard_map/ppermute | solution.py:37
  39.4 9.8 %collective-permute-start.13 = (bf16[2,112,768]{2,1,0:T(8,128)(2,1)S(1)}, bf16[2,112,768]{2,1,0:T(8,128)(2,1)S(1)}, u32[]{:S(2)}, u32[]{:S(2)}) collective-permute-start(bf16[2,112,768]{2,1,0:T(8,128)(2,1)S(1)} %get-tuple-element.36), channel_id=1, source_target_pairs={{0,4},{1,5},{2,6},{3,7},{4,8},{5,9},{6,10},{7,11},{8,12},{9,13},{1... | collective-permute-start | bytes 1032200 | tf_op jit(solution)/shard_map/ppermute | solution.py:37
  40.6 8.6 %collective-permute-start.10 = (bf16[32,3584]{1,0:T(8,128)(2,1)S(1)}, bf16[32,3584]{1,0:T(8,128)(2,1)S(1)}, u32[]{:S(2)}, u32[]{:S(2)}) collective-permute-start(bf16[32,3584]{1,0:T(8,128)(2,1)S(1)} %get-tuple-element.33), channel_id=1, source_target_pairs={{0,3},{1,0},{2,1},{3,2},{4,7},{5,4},{6,5},{7,6},{8,11},{9,8},{10,9... | collective-permute-start | bytes 688136 | tf_op jit(solution)/shard_map/ppermute | solution.py:37
  40.6 8.6 %collective-permute-start.11 = (bf16[32,3584]{1,0:T(8,128)(2,1)S(1)}, bf16[32,3584]{1,0:T(8,128)(2,1)S(1)}, u32[]{:S(2)}, u32[]{:S(2)}) collective-permute-start(bf16[32,3584]{1,0:T(8,128)(2,1)S(1)} %get-tuple-element.34), channel_id=1, source_target_pairs={{0,1},{1,2},{2,3},{3,0},{4,5},{5,6},{6,7},{7,4},{8,9},{9,10},{10,1... | collective-permute-start | bytes 688136 | tf_op jit(solution)/shard_map/ppermute | solution.py:37
  52.3 6.4 %collective-permute-start.17 = (bf16[256,256]{1,0:T(8,128)(2,1)S(1)}, bf16[256,256]{1,0:T(8,128)(2,1)S(1)}, u32[]{:S(2)}, u32[]{:S(2)}) collective-permute-start(bf16[256,256]{1,0:T(8,128)(2,1)S(1)} %get-tuple-element.41.a0), channel_id=1, source_target_pairs={{0,12},{1,13},{2,14},{3,15},{4,0},{5,1},{6,2},{7,3},{8,4},{9,5},{1... | collective-permute-start | bytes 393224 | tf_op jit(solution)/shard_map/ppermute | solution.py:37
  53.5 7.9 %collective-permute-start.16 = (bf16[256,256]{1,0:T(8,128)(2,1)S(1)}, bf16[256,256]{1,0:T(8,128)(2,1)S(1)}, u32[]{:S(2)}, u32[]{:S(2)}) collective-permute-start(bf16[256,256]{1,0:T(8,128)(2,1)S(1)} %get-tuple-element.41.a0), channel_id=1, source_target_pairs={{0,8},{1,9},{2,10},{3,11},{4,12},{5,13},{6,14},{7,15},{8,0},{9,1},... | collective-permute-start | bytes 393224 | tf_op jit(solution)/shard_map/ppermute | solution.py:37
  54.2 8.8 %collective-permute-start.18 = (bf16[256,256]{1,0:T(8,128)(2,1)S(1)}, bf16[256,256]{1,0:T(8,128)(2,1)S(1)}, u32[]{:S(2)}, u32[]{:S(2)}) collective-permute-start(bf16[256,256]{1,0:T(8,128)(2,1)S(1)} %get-tuple-element.41.a0), channel_id=1, source_target_pairs={{0,4},{1,5},{2,6},{3,7},{4,8},{5,9},{6,10},{7,11},{8,12},{9,13},{1... | collective-permute-start | bytes 393224 | tf_op jit(solution)/shard_map/ppermute | solution.py:37
  55.1 8.0 %collective-permute-start.19 = (bf16[256,256]{1,0:T(8,128)(2,1)S(1)}, bf16[256,256]{1,0:T(8,128)(2,1)S(1)}, u32[]{:S(2)}, u32[]{:S(2)}) collective-permute-start(bf16[256,256]{1,0:T(8,128)(2,1)S(1)} %get-tuple-element.41.a0), channel_id=1, source_target_pairs={{0,1},{1,0},{2,3},{3,2},{4,5},{5,4},{6,7},{7,6},{8,9},{9,8},{10,11... | collective-permute-start | bytes 393224 | tf_op jit(solution)/shard_map/ppermute | solution.py:37
  58.7 17.5 %collective-permute-start.26 = (bf16[256,256]{1,0:T(8,128)(2,1)S(1)}, bf16[256,256]{1,0:T(8,128)(2,1)S(1)}, u32[]{:S(2)}, u32[]{:S(2)}) collective-permute-start(bf16[256,256]{1,0:T(8,128)(2,1)S(1)} %collective-permute-done.17.a1), channel_id=1, source_target_pairs={{0,1},{1,0},{2,3},{3,2},{4,5},{5,4},{6,7},{7,6},{8,9},{9,8},{10,11... | collective-permute-start | bytes 393224 | tf_op jit(solution)/shard_map/ppermute | solution.py:37
  63.2 5.9 %collective-permute-start.20 = (bf16[64,256]{1,0:T(8,128)(2,1)S(1)}, bf16[64,256]{1,0:T(8,128)(2,1)S(1)}, u32[]{:S(2)}, u32[]{:S(2)}) collective-permute-start(bf16[64,256]{1,0:T(8,128)(2,1)S(1)} %get-tuple-element.45), channel_id=1, source_target_pairs={{0,2},{1,3},{2,0},{3,1},{4,6},{5,7},{6,4},{7,5},{8,10},{9,11},{10,... | collective-permute-start | bytes 98312 | tf_op jit(solution)/shard_map/ppermute | solution.py:37
  66.3 4.1 %collective-permute-start.21 = (bf16[64,256]{1,0:T(8,128)(2,1)S(1)}, bf16[64,256]{1,0:T(8,128)(2,1)S(1)}, u32[]{:S(2)}, u32[]{:S(2)}) collective-permute-start(bf16[64,256]{1,0:T(8,128)(2,1)S(1)} %get-tuple-element.46), channel_id=1, source_target_pairs={{0,1},{1,2},{2,3},{3,0},{4,5},{5,6},{6,7},{7,4},{8,9},{9,10},{10,1... | collective-permute-start | bytes 98312 | tf_op jit(solution)/shard_map/ppermute | solution.py:37
  67.1 5.1 %collective-permute-start.22 = (bf16[64,256]{1,0:T(8,128)(2,1)S(1)}, bf16[64,256]{1,0:T(8,128)(2,1)S(1)}, u32[]{:S(2)}, u32[]{:S(2)}) collective-permute-start(bf16[64,256]{1,0:T(8,128)(2,1)S(1)} %get-tuple-element.47), channel_id=1, source_target_pairs={{0,3},{1,0},{2,1},{3,2},{4,7},{5,4},{6,5},{7,6},{8,11},{9,8},{10,9... | collective-permute-start | bytes 98312 | tf_op jit(solution)/shard_map/ppermute | solution.py:37
  68.3 10.0 %collective-permute-start.27 = (bf16[256,256]{1,0:T(8,128)(2,1)S(1)}, bf16[256,256]{1,0:T(8,128)(2,1)S(1)}, u32[]{:S(2)}, u32[]{:S(2)}) collective-permute-start(bf16[256,256]{1,0:T(8,128)(2,1)S(1)} %collective-permute-done.16.a2), channel_id=1, source_target_pairs={{0,1},{1,0},{2,3},{3,2},{4,5},{5,4},{6,7},{7,6},{8,9},{9,8},{10,11... | collective-permute-start | bytes 393224 | tf_op jit(solution)/shard_map/ppermute | solution.py:37
  69.2 9.2 %collective-permute-start.28 = (bf16[256,256]{1,0:T(8,128)(2,1)S(1)}, bf16[256,256]{1,0:T(8,128)(2,1)S(1)}, u32[]{:S(2)}, u32[]{:S(2)}) collective-permute-start(bf16[256,256]{1,0:T(8,128)(2,1)S(1)} %collective-permute-done.18.a3), channel_id=1, source_target_pairs={{0,1},{1,0},{2,3},{3,2},{4,5},{5,4},{6,7},{7,6},{8,9},{9,8},{10,11... | collective-permute-start | bytes 393224 | tf_op jit(solution)/shard_map/ppermute | solution.py:37
  72.3 7.8 %collective-permute-start.23 = (bf16[64,768]{1,0:T(8,128)(2,1)S(1)}, bf16[64,768]{1,0:T(8,128)(2,1)S(1)}, u32[]{:S(2)}, u32[]{:S(2)}) collective-permute-start(bf16[64,768]{1,0:T(8,128)(2,1)S(1)} %cache_heads.1.after.c0), channel_id=1, source_target_pairs={{0,64},{1,65},{2,66},{3,67},{4,68},{5,69},{6,70},{7,71},{8,72},{9,... | collective-permute-start | bytes 294920 | tf_op jit(solution)/shard_map/ppermute | solution.py:37
  73.8 6.3 %collective-permute-start.24 = (bf16[64,768]{1,0:T(8,128)(2,1)S(1)}, bf16[64,768]{1,0:T(8,128)(2,1)S(1)}, u32[]{:S(2)}, u32[]{:S(2)}) collective-permute-start(bf16[64,768]{1,0:T(8,128)(2,1)S(1)} %cache_heads.1.after.c0), channel_id=1, source_target_pairs={{0,32},{1,33},{2,34},{3,35},{4,36},{5,37},{6,38},{7,39},{8,40},{9,... | collective-permute-start | bytes 294920 | tf_op jit(solution)/shard_map/ppermute | solution.py:37
  76.1 4.6 %collective-permute-start.25 = (bf16[64,768]{1,0:T(8,128)(2,1)S(1)}, bf16[64,768]{1,0:T(8,128)(2,1)S(1)}, u32[]{:S(2)}, u32[]{:S(2)}) collective-permute-start(bf16[64,768]{1,0:T(8,128)(2,1)S(1)} %cache_heads.1.after.c0), channel_id=1, source_target_pairs={{0,96},{1,97},{2,98},{3,99},{4,100},{5,101},{6,102},{7,103},{8,104... | collective-permute-start | bytes 294920 | tf_op jit(solution)/shard_map/ppermute | solution.py:37
  80.8 8.6 %collective-permute-start.29 = (bf16[4,64,768]{2,1,0:T(8,128)(2,1)S(1)}, bf16[4,64,768]{2,1,0:T(8,128)(2,1)S(1)}, u32[]{:S(2)}, u32[]{:S(2)}) collective-permute-start(bf16[4,64,768]{2,1,0:T(8,128)(2,1)S(1)} %cache_join.1.own), channel_id=1, source_target_pairs={{0,16},{1,17},{2,18},{3,19},{4,20},{5,21},{6,22},{7,23},{8,24},{9,... | collective-permute-start | bytes 1179656 | tf_op jit(solution)/shard_map/ppermute | solution.py:37
  80.9 6.0 %collective-permute-start.30 = (bf16[64,512]{1,0:T(8,128)(2,1)S(1)}, bf16[64,512]{1,0:T(8,128)(2,1)S(1)}, u32[]{:S(2)}, u32[]{:S(2)}) collective-permute-start(bf16[64,512]{1,0:T(8,128)(2,1)S(1)} %get-tuple-element.51), channel_id=1, source_target_pairs={{0,2},{1,3},{2,0},{3,1},{4,6},{5,7},{6,4},{7,5},{8,10},{9,11},{10,... | collective-permute-start | bytes 196616 | tf_op jit(solution)/shard_map/ppermute | solution.py:37
  82.2 4.7 %collective-permute-start.31 = (bf16[64,512]{1,0:T(8,128)(2,1)S(1)}, bf16[64,512]{1,0:T(8,128)(2,1)S(1)}, u32[]{:S(2)}, u32[]{:S(2)}) collective-permute-start(bf16[64,512]{1,0:T(8,128)(2,1)S(1)} %get-tuple-element.52), channel_id=1, source_target_pairs={{0,1},{1,2},{2,3},{3,0},{4,5},{5,6},{6,7},{7,4},{8,9},{9,10},{10,1... | collective-permute-start | bytes 196616 | tf_op jit(solution)/shard_map/ppermute | solution.py:37
  83.9 5.5 %collective-permute-start.32 = (bf16[64,512]{1,0:T(8,128)(2,1)S(1)}, bf16[64,512]{1,0:T(8,128)(2,1)S(1)}, u32[]{:S(2)}, u32[]{:S(2)}) collective-permute-start(bf16[64,512]{1,0:T(8,128)(2,1)S(1)} %get-tuple-element.53), channel_id=1, source_target_pairs={{0,3},{1,0},{2,1},{3,2},{4,7},{5,4},{6,5},{7,6},{8,11},{9,8},{10,9... | collective-permute-start | bytes 196616 | tf_op jit(solution)/shard_map/ppermute | solution.py:37
  (9 other events, 128.4 us)

commit v3 on v2

--- a/solution.py
+++ b/solution.py
@@ -124,7 +124,7 @@
     out[...] = jnp.concatenate([buf[k] for k in range(4)], axis=0).astype(jnp.bfloat16)
 
 
-def stage(s0, s2, s1, s3, after, block):
+def stage(s0, s2, s3, s1, after, block):
     for i, s in enumerate((s0, s1, s2, s3)):
         block[i] = s[...]
 
@@ -344,7 +344,7 @@
     (s0,) = call(
         stage,
         [((4, 112, COLS), bf)],
-        (w0, *spread(lambda j: send(w0, along_first(-j))), n0),
+        (w0, *[send(w0, along_first(-j)) for j in (2, 3, 1)], n0),
         [VM] * 4 + [ANY],
     )
     n1 = send(n0, along_x(-1))

time: 91.4 us -> 91.8 us (level)
  starting transfers between devices: 41.6 us -> 42.9 us
    ppermute x33, starting transfers between devices: 41.6 us -> 42.9 us  [send(): return lax.ppermute(v, EVERY, [(flat(*p), flat(*move(*p))) for p in PLACES])]
where the time goes in v3:
time: 91.8 us; the launch traced here: 91.5 us
  starting transfers between devices  42.9 us (47%)
  waiting for transfers between devices  34.5 us (38%)
  Pallas kernels  10.6 us (12%)
  local copies, waits for them, and re-layouts  2.57 us (3%)
    ppermute x33, starting transfers between devices, send(): return lax.ppermute(v, EVERY, [(flat(*p), flat(*move(*p))) for p in PLACES])  42.9 us
    ppermute x33, waiting for transfers between devices, send(): return lax.ppermute(v, EVERY, [(flat(*p), flat(*move(*p))) for p in PLACES])  34.5 us
    pallas_call x16, Pallas kernels, call(): pl.pallas_call(kernel, out_shape=outs, in_specs=[VM] * len(operands) if i...  10.6 us
    unnamed x16, local copies, waits for them, and re-layouts  2.57 us
  transfers between devices with their start and end apart: 33, of which 15 were waited for; matrix products, arithmetic and copies ran while one was open for 0% of the time, Pallas kernels for 7%

profile of v3, /device:TPU:6, one launch (start us, length us, event | category | flops | bytes accessed | tf_op | source)
XLA Modules:
  0.0 91.5 jit_solution(3020077104031573619)
XLA Ops:
  0.6 1.6 %cut.1 = (bf16[28,768]{1,0:T(8,128)(2,1)}, bf16[28,768]{1,0:T(8,128)(2,1)}, bf16[28,768]{1,0:T(8,128)(2,1)}, bf16[28,768]{1,0:T(8,128)(2,1)}) custom-call(bf16[28,2048]{1,0:T(8,128)(2,1)} %wq.1, bf16[28,768]{1,0:T(8,128)(2,1)} %wkv.1), custom_call_target="tpu_custom_call" | custom-call | tf_op jit(solution)/shard_map/cut/pallas_call | solution.py:77
  2.2 1.5 %collective-permute-start = (bf16[28,768]{1,0:T(8,128)(2,1)}, bf16[28,768]{1,0:T(8,128)(2,1)S(1)}, u32[]{:S(2)}, u32[]{:S(2)}) collective-permute-start(bf16[28,768]{1,0:T(8,128)(2,1)} %get-tuple-element.29), channel_id=1, source_target_pairs={{0,2},{1,3},{2,0},{3,1},{4,6},{5,7},{6,4},{7,5},{8,10},{9,11},{10,... | collective-permute-start | bytes 129032 | tf_op jit(solution)/shard_map/ppermute | solution.py:37
  3.7 2.1 %collective-permute-start.1 = (bf16[28,768]{1,0:T(8,128)(2,1)}, bf16[28,768]{1,0:T(8,128)(2,1)S(1)}, u32[]{:S(2)}, u32[]{:S(2)}) collective-permute-start(bf16[28,768]{1,0:T(8,128)(2,1)} %get-tuple-element.30), channel_id=1, source_target_pairs={{0,1},{1,2},{2,3},{3,0},{4,5},{5,6},{6,7},{7,4},{8,9},{9,10},{10,1... | collective-permute-start | bytes 129032 | tf_op jit(solution)/shard_map/ppermute | solution.py:37
  6.7 1.6 %collective-permute-done.p2 = bf16[28,768]{1,0:T(8,128)(2,1)S(1)} collective-permute-done((bf16[28,768]{1,0:T(8,128)(2,1)}, bf16[28,768]{1,0:T(8,128)(2,1)S(1)}, u32[]{:S(2)}, u32[]{:S(2)}) %collective-permute-start) | collective-permute-done | bytes 43040 | tf_op jit(solution)/shard_map/ppermute | solution.py:37
  8.3 3.0 %collective-permute-done.2.p3 = bf16[28,768]{1,0:T(8,128)(2,1)S(1)} collective-permute-done((bf16[28,768]{1,0:T(8,128)(2,1)}, bf16[28,768]{1,0:T(8,128)(2,1)S(1)}, u32[]{:S(2)}, u32[]{:S(2)}) %collective-permute-start.2) | collective-permute-done | bytes 43040 | tf_op jit(solution)/shard_map/ppermute | solution.py:37
  11.4 4.0 %collective-permute-start.5 = (bf16[112,768]{1,0:T(8,128)(2,1)S(1)}, bf16[112,768]{1,0:T(8,128)(2,1)S(1)}, u32[]{:S(2)}, u32[]{:S(2)}) collective-permute-start(bf16[112,768]{1,0:T(8,128)(2,1)S(1)} %place.1.after.s0), channel_id=1, source_target_pairs={{0,64},{1,65},{2,66},{3,67},{4,68},{5,69},{6,70},{7,71},{8,72},{9,... | collective-permute-start | bytes 516104 | tf_op jit(solution)/shard_map/ppermute | solution.py:37
  16.4 2.2 %collective-permute-start.7 = (bf16[112,768]{1,0:T(8,128)(2,1)S(1)}, bf16[112,768]{1,0:T(8,128)(2,1)S(1)}, u32[]{:S(2)}, u32[]{:S(2)}) collective-permute-start(bf16[112,768]{1,0:T(8,128)(2,1)S(1)} %place.1.after.s0), channel_id=1, source_target_pairs={{0,96},{1,97},{2,98},{3,99},{4,100},{5,101},{6,102},{7,103},{8,104... | collective-permute-start | bytes 516104 | tf_op jit(solution)/shard_map/ppermute | solution.py:37
  20.6 1.4 %collective-permute-done.6.s3 = bf16[112,768]{1,0:T(8,128)(2,1)S(1)} collective-permute-done((bf16[112,768]{1,0:T(8,128)(2,1)S(1)}, bf16[112,768]{1,0:T(8,128)(2,1)S(1)}, u32[]{:S(2)}, u32[]{:S(2)}) %collective-permute-start.6) | collective-permute-done | bytes 172064 | tf_op jit(solution)/shard_map/ppermute | solution.py:37
  22.6 3.2 %collective-permute-start.8 = (bf16[4,112,768]{2,1,0:T(8,128)(2,1)S(1)}, bf16[4,112,768]{2,1,0:T(8,128)(2,1)S(1)}, u32[]{:S(2)}, u32[]{:S(2)}) collective-permute-start(bf16[4,112,768]{2,1,0:T(8,128)(2,1)S(1)} %stage.1.s0), channel_id=1, source_target_pairs={{0,12},{1,13},{2,14},{3,15},{4,0},{5,1},{6,2},{7,3},{8,4},{9,5},{1... | collective-permute-start | bytes 2064392 | tf_op jit(solution)/shard_map/ppermute | solution.py:37
  25.7 3.2 %collective-permute-start.4 = (bf16[64,3584]{1,0:T(8,128)(2,1)S(1)}, bf16[64,3584]{1,0:T(8,128)(2,1)S(1)}, u32[]{:S(2)}, u32[]{:S(2)}) collective-permute-start(bf16[64,3584]{1,0:T(8,128)(2,1)S(1)} %norm.1.after.n0), channel_id=1, source_target_pairs={{0,1},{1,2},{2,3},{3,0},{4,5},{5,6},{6,7},{7,4},{8,9},{9,10},{10,1... | collective-permute-start | bytes 1376264 | tf_op jit(solution)/shard_map/ppermute | solution.py:37
  29.0 6.9 %collective-permute-done.3.n1 = bf16[64,3584]{1,0:T(8,128)(2,1)S(1)} collective-permute-done((bf16[64,3584]{1,0:T(8,128)(2,1)S(1)}, bf16[64,3584]{1,0:T(8,128)(2,1)S(1)}, u32[]{:S(2)}, u32[]{:S(2)}) %collective-permute-start.3) | collective-permute-done | bytes 458784 | tf_op jit(solution)/shard_map/ppermute | solution.py:37
  35.9 2.0 %collective-permute-done.9.s3 = bf16[4,112,768]{2,1,0:T(8,128)(2,1)S(1)} collective-permute-done((bf16[4,112,768]{2,1,0:T(8,128)(2,1)S(1)}, bf16[4,112,768]{2,1,0:T(8,128)(2,1)S(1)}, u32[]{:S(2)}, u32[]{:S(2)}) %collective-permute-start.9) | collective-permute-done | bytes 688160 | tf_op jit(solution)/shard_map/ppermute | solution.py:37
  40.3 3.2 %collective-permute-start.11 = (bf16[32,3584]{1,0:T(8,128)(2,1)S(1)}, bf16[32,3584]{1,0:T(8,128)(2,1)S(1)}, u32[]{:S(2)}, u32[]{:S(2)}) collective-permute-start(bf16[32,3584]{1,0:T(8,128)(2,1)S(1)} %get-tuple-element.34), channel_id=1, source_target_pairs={{0,1},{1,2},{2,3},{3,0},{4,5},{5,6},{6,7},{7,4},{8,9},{9,10},{10,1... | collective-permute-start | bytes 688136 | tf_op jit(solution)/shard_map/ppermute | solution.py:37
  43.5 6.3 %collective-permute-done.10.after1.n2a = bf16[32,3584]{1,0:T(8,128)(2,1)S(1)} collective-permute-done((bf16[32,3584]{1,0:T(8,128)(2,1)S(1)}, bf16[32,3584]{1,0:T(8,128)(2,1)S(1)}, u32[]{:S(2)}, u32[]{:S(2)}) %collective-permute-start.10) | collective-permute-done | bytes 229408 | tf_op jit(solution)/shard_map/ppermute | solution.py:37
  50.0 1.4 %gather.1 = (bf16[32,112,768]{2,1,0:T(8,128)(2,1)S(1)}, bf16[256,3584]{1,0:T(8,128)(2,1)S(1)}, f32[256,128]{1,0:T(8,128)S(1)}, f32[512]{0:T(512)S(1)}, f32[2,128]{1,0:T(2,128)S(1)}) custom-call(s32[8,16]{1,0:T(8,128)S(1)} %copy-done.3, bf16[12,112,768]{2,1,0:T(8,128)(2,1)S(1)} %get-tuple-element.32.own1, bf16[4,112,768]{2,1,0:T(8,128)(2,1)S(1)} %join2.1.own2, ...), custom_call_target="tpu_custom_call" | custom-call | tf_op jit(solution)/shard_map/gather/pallas_call | solution.py:77
  52.9 1.3 %collective-permute-start.17 = (bf16[256,256]{1,0:T(8,128)(2,1)S(1)}, bf16[256,256]{1,0:T(8,128)(2,1)S(1)}, u32[]{:S(2)}, u32[]{:S(2)}) collective-permute-start(bf16[256,256]{1,0:T(8,128)(2,1)S(1)} %get-tuple-element.41.a0), channel_id=1, source_target_pairs={{0,12},{1,13},{2,14},{3,15},{4,0},{5,1},{6,2},{7,3},{8,4},{9,5},{1... | collective-permute-start | bytes 393224 | tf_op jit(solution)/shard_map/ppermute | solution.py:37
  56.2 3.0 %collective-permute-done.17.a1 = bf16[256,256]{1,0:T(8,128)(2,1)S(1)} collective-permute-done((bf16[256,256]{1,0:T(8,128)(2,1)S(1)}, bf16[256,256]{1,0:T(8,128)(2,1)S(1)}, u32[]{:S(2)}, u32[]{:S(2)}) %collective-permute-start.17) | collective-permute-done | bytes 131104 | tf_op jit(solution)/shard_map/ppermute | solution.py:37
  59.3 1.9 %collective-permute-start.26 = (bf16[256,256]{1,0:T(8,128)(2,1)S(1)}, bf16[256,256]{1,0:T(8,128)(2,1)S(1)}, u32[]{:S(2)}, u32[]{:S(2)}) collective-permute-start(bf16[256,256]{1,0:T(8,128)(2,1)S(1)} %collective-permute-done.17.a1), channel_id=1, source_target_pairs={{0,1},{1,0},{2,3},{3,2},{4,5},{5,4},{6,7},{7,6},{8,9},{9,8},{10,11... | collective-permute-start | bytes 393224 | tf_op jit(solution)/shard_map/ppermute | solution.py:37
  61.2 1.4 %q_project.1.after1.q = bf16[256,512]{1,0:T(8,128)(2,1)S(1)} custom-call(bf16[32,112,768]{2,1,0:T(8,128)(2,1)S(1)} %get-tuple-element.42.w, bf16[256,3584]{1,0:T(8,128)(2,1)S(1)} %get-tuple-element.38.x_in, f32[256,128]{1,0:T(8,128)S(1)} %get-tuple-element.39.cs, f32[512]{0:T(512)S(1)} %get-tuple-element.43.qb), custom_call_target="tpu_custom_call" | custom-call | tf_op jit(solution)/shard_map/q_project/pallas_call | solution.py:77
  63.9 2.8 %collective-permute-start.20 = (bf16[64,256]{1,0:T(8,128)(2,1)S(1)}, bf16[64,256]{1,0:T(8,128)(2,1)S(1)}, u32[]{:S(2)}, u32[]{:S(2)}) collective-permute-start(bf16[64,256]{1,0:T(8,128)(2,1)S(1)} %get-tuple-element.45), channel_id=1, source_target_pairs={{0,2},{1,3},{2,0},{3,1},{4,6},{5,7},{6,4},{7,5},{8,10},{9,11},{10,... | collective-permute-start | bytes 98312 | tf_op jit(solution)/shard_map/ppermute | solution.py:37
  67.5 1.1 %collective-permute-start.22 = (bf16[64,256]{1,0:T(8,128)(2,1)S(1)}, bf16[64,256]{1,0:T(8,128)(2,1)S(1)}, u32[]{:S(2)}, u32[]{:S(2)}) collective-permute-start(bf16[64,256]{1,0:T(8,128)(2,1)S(1)} %get-tuple-element.47), channel_id=1, source_target_pairs={{0,3},{1,0},{2,1},{3,2},{4,7},{5,4},{6,5},{7,6},{8,11},{9,8},{10,9... | collective-permute-start | bytes 98312 | tf_op jit(solution)/shard_map/ppermute | solution.py:37
  68.7 1.1 %collective-permute-start.27 = (bf16[256,256]{1,0:T(8,128)(2,1)S(1)}, bf16[256,256]{1,0:T(8,128)(2,1)S(1)}, u32[]{:S(2)}, u32[]{:S(2)}) collective-permute-start(bf16[256,256]{1,0:T(8,128)(2,1)S(1)} %collective-permute-done.16.a2), channel_id=1, source_target_pairs={{0,1},{1,0},{2,3},{3,2},{4,5},{5,4},{6,7},{7,6},{8,9},{9,8},{10,11... | collective-permute-start | bytes 393224 | tf_op jit(solution)/shard_map/ppermute | solution.py:37
  70.9 1.8 %collective-permute-done.22.t3 = bf16[64,256]{1,0:T(8,128)(2,1)S(1)} collective-permute-done((bf16[64,256]{1,0:T(8,128)(2,1)S(1)}, bf16[64,256]{1,0:T(8,128)(2,1)S(1)}, u32[]{:S(2)}, u32[]{:S(2)}) %collective-permute-start.22) | collective-permute-done | bytes 32800 | tf_op jit(solution)/shard_map/ppermute | solution.py:37
  72.7 1.5 %collective-permute-start.23 = (bf16[64,768]{1,0:T(8,128)(2,1)S(1)}, bf16[64,768]{1,0:T(8,128)(2,1)S(1)}, u32[]{:S(2)}, u32[]{:S(2)}) collective-permute-start(bf16[64,768]{1,0:T(8,128)(2,1)S(1)} %cache_heads.1.after.c0), channel_id=1, source_target_pairs={{0,64},{1,65},{2,66},{3,67},{4,68},{5,69},{6,70},{7,71},{8,72},{9,... | collective-permute-start | bytes 294920 | tf_op jit(solution)/shard_map/ppermute | solution.py:37
  74.3 2.3 %collective-permute-start.24 = (bf16[64,768]{1,0:T(8,128)(2,1)S(1)}, bf16[64,768]{1,0:T(8,128)(2,1)S(1)}, u32[]{:S(2)}, u32[]{:S(2)}) collective-permute-start(bf16[64,768]{1,0:T(8,128)(2,1)S(1)} %cache_heads.1.after.c0), channel_id=1, source_target_pairs={{0,32},{1,33},{2,34},{3,35},{4,36},{5,37},{6,38},{7,39},{8,40},{9,... | collective-permute-start | bytes 294920 | tf_op jit(solution)/shard_map/ppermute | solution.py:37
  77.5 1.2 %attend_own.1 = (f32[256,1024]{1,0:T(8,128)S(1)}, bf16[256,128]{1,0:T(8,128)(2,1)S(1)}) custom-call(s32[8,16]{1,0:T(8,128)S(1)} %copy-done.3, bf16[256,512]{1,0:T(8,128)(2,1)S(1)} %q_project.1.after1.q, bf16[256,256]{1,0:T(8,128)(2,1)S(1)} %get-tuple-element.41.a0, bf16[256,256]{1,0:T(8,128)(2,1)S(1)} %collective-permute-done.17.a1, ...), custom_call_target="tpu_custom_call" | custom-call | tf_op jit(solution)/shard_map/attend_own/pallas_call | solution.py:77
  78.8 1.7 %attend.1 = (bf16[64,512]{1,0:T(8,128)(2,1)S(1)}, bf16[64,512]{1,0:T(8,128)(2,1)S(1)}, bf16[64,512]{1,0:T(8,128)(2,1)S(1)}, bf16[64,512]{1,0:T(8,128)(2,1)S(1)}) custom-call(f32[256,1024]{1,0:T(8,128)S(1)} %get-tuple-element.48.mask, bf16[256,128]{1,0:T(8,128)(2,1)S(1)} %get-tuple-element.49.last, bf16[256,512]{1,0:T(8,128)(2,1)S(1)} %q_project.1.after1.q, ...), custom_call_target="tpu_custom_call" | custom-call | tf_op jit(solution)/shard_map/attend/pallas_call | solution.py:77
  81.4 1.2 %collective-permute-start.30 = (bf16[64,512]{1,0:T(8,128)(2,1)S(1)}, bf16[64,512]{1,0:T(8,128)(2,1)S(1)}, u32[]{:S(2)}, u32[]{:S(2)}) collective-permute-start(bf16[64,512]{1,0:T(8,128)(2,1)S(1)} %get-tuple-element.51), channel_id=1, source_target_pairs={{0,2},{1,3},{2,0},{3,1},{4,6},{5,7},{6,4},{7,5},{8,10},{9,11},{10,... | collective-permute-start | bytes 196616 | tf_op jit(solution)/shard_map/ppermute | solution.py:37
  82.6 1.8 %collective-permute-start.31 = (bf16[64,512]{1,0:T(8,128)(2,1)S(1)}, bf16[64,512]{1,0:T(8,128)(2,1)S(1)}, u32[]{:S(2)}, u32[]{:S(2)}) collective-permute-start(bf16[64,512]{1,0:T(8,128)(2,1)S(1)} %get-tuple-element.52), channel_id=1, source_target_pairs={{0,1},{1,2},{2,3},{3,0},{4,5},{5,6},{6,7},{7,4},{8,9},{9,10},{10,1... | collective-permute-start | bytes 196616 | tf_op jit(solution)/shard_map/ppermute | solution.py:37
  84.6 2.8 %collective-permute-done.30.r2 = bf16[64,512]{1,0:T(8,128)(2,1)S(1)} collective-permute-done((bf16[64,512]{1,0:T(8,128)(2,1)S(1)}, bf16[64,512]{1,0:T(8,128)(2,1)S(1)}, u32[]{:S(2)}, u32[]{:S(2)}) %collective-permute-start.30) | collective-permute-done | bytes 65568 | tf_op jit(solution)/shard_map/ppermute | solution.py:37
  87.4 2.4 %collective-permute-done.32.r3 = bf16[64,512]{1,0:T(8,128)(2,1)S(1)} collective-permute-done((bf16[64,512]{1,0:T(8,128)(2,1)S(1)}, bf16[64,512]{1,0:T(8,128)(2,1)S(1)}, u32[]{:S(2)}, u32[]{:S(2)}) %collective-permute-start.32) | collective-permute-done | bytes 65568 | tf_op jit(solution)/shard_map/ppermute | solution.py:37
  89.8 1.7 %finish.1 = (bf16[64,2048]{1,0:T(8,128)(2,1)}, bf16[1,1,512,768]{3,2,1,0:T(8,128)(2,1)}) custom-call(s32[8,16]{1,0:T(8,128)S(1)} %copy-done.7, bf16[4,64,768]{2,1,0:T(8,128)(2,1)S(1)} %cache_join.1.own, bf16[4,64,768]{2,1,0:T(8,128)(2,1)S(1)} %collective-permute-done.29.other, bf16[64,512]{1,0:T(8,128)(2,1)S(1)} %get-tuple-element.50.after.r0, ...), custom_call_target="tpu_custom_call" | custom-call | tf_op jit(solution)/shard_map/finish/pallas_call | solution.py:77
  (66 shorter events, 15.9 us)
Async XLA Ops:
  2.2 6.1 %collective-permute-start = (bf16[28,768]{1,0:T(8,128)(2,1)}, bf16[28,768]{1,0:T(8,128)(2,1)S(1)}, u32[]{:S(2)}, u32[]{:S(2)}) collective-permute-start(bf16[28,768]{1,0:T(8,128)(2,1)} %get-tuple-element.29), channel_id=1, source_target_pairs={{0,2},{1,3},{2,0},{3,1},{4,6},{5,7},{6,4},{7,5},{8,10},{9,11},{10,... | collective-permute-start | bytes 129032 | tf_op jit(solution)/shard_map/ppermute | solution.py:37
  3.7 4.6 %collective-permute-start.1 = (bf16[28,768]{1,0:T(8,128)(2,1)}, bf16[28,768]{1,0:T(8,128)(2,1)S(1)}, u32[]{:S(2)}, u32[]{:S(2)}) collective-permute-start(bf16[28,768]{1,0:T(8,128)(2,1)} %get-tuple-element.30), channel_id=1, source_target_pairs={{0,1},{1,2},{2,3},{3,0},{4,5},{5,6},{6,7},{7,4},{8,9},{9,10},{10,1... | collective-permute-start | bytes 129032 | tf_op jit(solution)/shard_map/ppermute | solution.py:37
  5.8 5.5 %collective-permute-start.2 = (bf16[28,768]{1,0:T(8,128)(2,1)}, bf16[28,768]{1,0:T(8,128)(2,1)S(1)}, u32[]{:S(2)}, u32[]{:S(2)}) collective-permute-start(bf16[28,768]{1,0:T(8,128)(2,1)} %get-tuple-element.31), channel_id=1, source_target_pairs={{0,3},{1,0},{2,1},{3,2},{4,7},{5,4},{6,5},{7,6},{8,11},{9,8},{10,9... | collective-permute-start | bytes 129032 | tf_op jit(solution)/shard_map/ppermute | solution.py:37
  11.4 9.1 %collective-permute-start.5 = (bf16[112,768]{1,0:T(8,128)(2,1)S(1)}, bf16[112,768]{1,0:T(8,128)(2,1)S(1)}, u32[]{:S(2)}, u32[]{:S(2)}) collective-permute-start(bf16[112,768]{1,0:T(8,128)(2,1)S(1)} %place.1.after.s0), channel_id=1, source_target_pairs={{0,64},{1,65},{2,66},{3,67},{4,68},{5,69},{6,70},{7,71},{8,72},{9,... | collective-permute-start | bytes 516104 | tf_op jit(solution)/shard_map/ppermute | solution.py:37
  15.4 6.6 %collective-permute-start.6 = (bf16[112,768]{1,0:T(8,128)(2,1)S(1)}, bf16[112,768]{1,0:T(8,128)(2,1)S(1)}, u32[]{:S(2)}, u32[]{:S(2)}) collective-permute-start(bf16[112,768]{1,0:T(8,128)(2,1)S(1)} %place.1.after.s0), channel_id=1, source_target_pairs={{0,32},{1,33},{2,34},{3,35},{4,36},{5,37},{6,38},{7,39},{8,40},{9,... | collective-permute-start | bytes 516104 | tf_op jit(solution)/shard_map/ppermute | solution.py:37
  16.4 6.1 %collective-permute-start.7 = (bf16[112,768]{1,0:T(8,128)(2,1)S(1)}, bf16[112,768]{1,0:T(8,128)(2,1)S(1)}, u32[]{:S(2)}, u32[]{:S(2)}) collective-permute-start(bf16[112,768]{1,0:T(8,128)(2,1)S(1)} %place.1.after.s0), channel_id=1, source_target_pairs={{0,96},{1,97},{2,98},{3,99},{4,100},{5,101},{6,102},{7,103},{8,104... | collective-permute-start | bytes 516104 | tf_op jit(solution)/shard_map/ppermute | solution.py:37
  22.6 13.3 %collective-permute-start.8 = (bf16[4,112,768]{2,1,0:T(8,128)(2,1)S(1)}, bf16[4,112,768]{2,1,0:T(8,128)(2,1)S(1)}, u32[]{:S(2)}, u32[]{:S(2)}) collective-permute-start(bf16[4,112,768]{2,1,0:T(8,128)(2,1)S(1)} %stage.1.s0), channel_id=1, source_target_pairs={{0,12},{1,13},{2,14},{3,15},{4,0},{5,1},{6,2},{7,3},{8,4},{9,5},{1... | collective-permute-start | bytes 2064392 | tf_op jit(solution)/shard_map/ppermute | solution.py:37
  25.7 12.1 %collective-permute-start.9 = (bf16[4,112,768]{2,1,0:T(8,128)(2,1)S(1)}, bf16[4,112,768]{2,1,0:T(8,128)(2,1)S(1)}, u32[]{:S(2)}, u32[]{:S(2)}) collective-permute-start(bf16[4,112,768]{2,1,0:T(8,128)(2,1)S(1)} %stage.1.s0), channel_id=1, source_target_pairs={{0,4},{1,5},{2,6},{3,7},{4,8},{5,9},{6,10},{7,11},{8,12},{9,13},{1... | collective-permute-start | bytes 2064392 | tf_op jit(solution)/shard_map/ppermute | solution.py:37
  25.7 10.1 %collective-permute-start.3 = (bf16[64,3584]{1,0:T(8,128)(2,1)S(1)}, bf16[64,3584]{1,0:T(8,128)(2,1)S(1)}, u32[]{:S(2)}, u32[]{:S(2)}) collective-permute-start(bf16[64,3584]{1,0:T(8,128)(2,1)S(1)} %norm.1.after.n0), channel_id=1, source_target_pairs={{0,3},{1,0},{2,1},{3,2},{4,7},{5,4},{6,5},{7,6},{8,11},{9,8},{10,9... | collective-permute-start | bytes 1376264 | tf_op jit(solution)/shard_map/ppermute | solution.py:37
  25.7 10.1 %collective-permute-start.4 = (bf16[64,3584]{1,0:T(8,128)(2,1)S(1)}, bf16[64,3584]{1,0:T(8,128)(2,1)S(1)}, u32[]{:S(2)}, u32[]{:S(2)}) collective-permute-start(bf16[64,3584]{1,0:T(8,128)(2,1)S(1)} %norm.1.after.n0), channel_id=1, source_target_pairs={{0,1},{1,2},{2,3},{3,0},{4,5},{5,6},{6,7},{7,4},{8,9},{9,10},{10,1... | collective-permute-start | bytes 1376264 | tf_op jit(solution)/shard_map/ppermute | solution.py:37
  38.1 11.9 %collective-permute-start.14 = (bf16[12,112,768]{2,1,0:T(8,128)(2,1)S(1)}, bf16[12,112,768]{2,1,0:T(8,128)(2,1)S(1)}, u32[]{:S(2)}, u32[]{:S(2)}) collective-permute-start(bf16[12,112,768]{2,1,0:T(8,128)(2,1)S(1)} %get-tuple-element.32.own1), channel_id=1, source_target_pairs={{0,16},{1,17},{2,18},{3,19},{4,20},{5,21},{6,22},{7,23},{8,24},{9,... | collective-permute-start | bytes 6193160 | tf_op jit(solution)/shard_map/ppermute | solution.py:37
  38.2 11.6 %collective-permute-start.12 = (bf16[2,112,768]{2,1,0:T(8,128)(2,1)S(1)}, bf16[2,112,768]{2,1,0:T(8,128)(2,1)S(1)}, u32[]{:S(2)}, u32[]{:S(2)}) collective-permute-start(bf16[2,112,768]{2,1,0:T(8,128)(2,1)S(1)} %get-tuple-element.35), channel_id=1, source_target_pairs={{0,12},{1,13},{2,14},{3,15},{4,0},{5,1},{6,2},{7,3},{8,4},{9,5},{1... | collective-permute-start | bytes 1032200 | tf_op jit(solution)/shard_map/ppermute | solution.py:37
  39.2 10.6 %collective-permute-start.13 = (bf16[2,112,768]{2,1,0:T(8,128)(2,1)S(1)}, bf16[2,112,768]{2,1,0:T(8,128)(2,1)S(1)}, u32[]{:S(2)}, u32[]{:S(2)}) collective-permute-start(bf16[2,112,768]{2,1,0:T(8,128)(2,1)S(1)} %get-tuple-element.36), channel_id=1, source_target_pairs={{0,4},{1,5},{2,6},{3,7},{4,8},{5,9},{6,10},{7,11},{8,12},{9,13},{1... | collective-permute-start | bytes 1032200 | tf_op jit(solution)/shard_map/ppermute | solution.py:37
  40.3 9.5 %collective-permute-start.10 = (bf16[32,3584]{1,0:T(8,128)(2,1)S(1)}, bf16[32,3584]{1,0:T(8,128)(2,1)S(1)}, u32[]{:S(2)}, u32[]{:S(2)}) collective-permute-start(bf16[32,3584]{1,0:T(8,128)(2,1)S(1)} %get-tuple-element.33), channel_id=1, source_target_pairs={{0,3},{1,0},{2,1},{3,2},{4,7},{5,4},{6,5},{7,6},{8,11},{9,8},{10,9... | collective-permute-start | bytes 688136 | tf_op jit(solution)/shard_map/ppermute | solution.py:37
  40.3 9.5 %collective-permute-start.11 = (bf16[32,3584]{1,0:T(8,128)(2,1)S(1)}, bf16[32,3584]{1,0:T(8,128)(2,1)S(1)}, u32[]{:S(2)}, u32[]{:S(2)}) collective-permute-start(bf16[32,3584]{1,0:T(8,128)(2,1)S(1)} %get-tuple-element.34), channel_id=1, source_target_pairs={{0,1},{1,2},{2,3},{3,0},{4,5},{5,6},{6,7},{7,4},{8,9},{9,10},{10,1... | collective-permute-start | bytes 688136 | tf_op jit(solution)/shard_map/ppermute | solution.py:37
  52.9 6.4 %collective-permute-start.17 = (bf16[256,256]{1,0:T(8,128)(2,1)S(1)}, bf16[256,256]{1,0:T(8,128)(2,1)S(1)}, u32[]{:S(2)}, u32[]{:S(2)}) collective-permute-start(bf16[256,256]{1,0:T(8,128)(2,1)S(1)} %get-tuple-element.41.a0), channel_id=1, source_target_pairs={{0,12},{1,13},{2,14},{3,15},{4,0},{5,1},{6,2},{7,3},{8,4},{9,5},{1... | collective-permute-start | bytes 393224 | tf_op jit(solution)/shard_map/ppermute | solution.py:37
  54.2 8.4 %collective-permute-start.16 = (bf16[256,256]{1,0:T(8,128)(2,1)S(1)}, bf16[256,256]{1,0:T(8,128)(2,1)S(1)}, u32[]{:S(2)}, u32[]{:S(2)}) collective-permute-start(bf16[256,256]{1,0:T(8,128)(2,1)S(1)} %get-tuple-element.41.a0), channel_id=1, source_target_pairs={{0,8},{1,9},{2,10},{3,11},{4,12},{5,13},{6,14},{7,15},{8,0},{9,1},... | collective-permute-start | bytes 393224 | tf_op jit(solution)/shard_map/ppermute | solution.py:37
  54.2 9.4 %collective-permute-start.18 = (bf16[256,256]{1,0:T(8,128)(2,1)S(1)}, bf16[256,256]{1,0:T(8,128)(2,1)S(1)}, u32[]{:S(2)}, u32[]{:S(2)}) collective-permute-start(bf16[256,256]{1,0:T(8,128)(2,1)S(1)} %get-tuple-element.41.a0), channel_id=1, source_target_pairs={{0,4},{1,5},{2,6},{3,7},{4,8},{5,9},{6,10},{7,11},{8,12},{9,13},{1... | collective-permute-start | bytes 393224 | tf_op jit(solution)/shard_map/ppermute | solution.py:37
  55.1 8.6 %collective-permute-start.19 = (bf16[256,256]{1,0:T(8,128)(2,1)S(1)}, bf16[256,256]{1,0:T(8,128)(2,1)S(1)}, u32[]{:S(2)}, u32[]{:S(2)}) collective-permute-start(bf16[256,256]{1,0:T(8,128)(2,1)S(1)} %get-tuple-element.41.a0), channel_id=1, source_target_pairs={{0,1},{1,0},{2,3},{3,2},{4,5},{5,4},{6,7},{7,6},{8,9},{9,8},{10,11... | collective-permute-start | bytes 393224 | tf_op jit(solution)/shard_map/ppermute | solution.py:37
  59.3 17.3 %collective-permute-start.26 = (bf16[256,256]{1,0:T(8,128)(2,1)S(1)}, bf16[256,256]{1,0:T(8,128)(2,1)S(1)}, u32[]{:S(2)}, u32[]{:S(2)}) collective-permute-start(bf16[256,256]{1,0:T(8,128)(2,1)S(1)} %collective-permute-done.17.a1), channel_id=1, source_target_pairs={{0,1},{1,0},{2,3},{3,2},{4,5},{5,4},{6,7},{7,6},{8,9},{9,8},{10,11... | collective-permute-start | bytes 393224 | tf_op jit(solution)/shard_map/ppermute | solution.py:37
  63.9 5.9 %collective-permute-start.20 = (bf16[64,256]{1,0:T(8,128)(2,1)S(1)}, bf16[64,256]{1,0:T(8,128)(2,1)S(1)}, u32[]{:S(2)}, u32[]{:S(2)}) collective-permute-start(bf16[64,256]{1,0:T(8,128)(2,1)S(1)} %get-tuple-element.45), channel_id=1, source_target_pairs={{0,2},{1,3},{2,0},{3,1},{4,6},{5,7},{6,4},{7,5},{8,10},{9,11},{10,... | collective-permute-start | bytes 98312 | tf_op jit(solution)/shard_map/ppermute | solution.py:37
  66.7 4.3 %collective-permute-start.21 = (bf16[64,256]{1,0:T(8,128)(2,1)S(1)}, bf16[64,256]{1,0:T(8,128)(2,1)S(1)}, u32[]{:S(2)}, u32[]{:S(2)}) collective-permute-start(bf16[64,256]{1,0:T(8,128)(2,1)S(1)} %get-tuple-element.46), channel_id=1, source_target_pairs={{0,1},{1,2},{2,3},{3,0},{4,5},{5,6},{6,7},{7,4},{8,9},{9,10},{10,1... | collective-permute-start | bytes 98312 | tf_op jit(solution)/shard_map/ppermute | solution.py:37
  67.5 5.1 %collective-permute-start.22 = (bf16[64,256]{1,0:T(8,128)(2,1)S(1)}, bf16[64,256]{1,0:T(8,128)(2,1)S(1)}, u32[]{:S(2)}, u32[]{:S(2)}) collective-permute-start(bf16[64,256]{1,0:T(8,128)(2,1)S(1)} %get-tuple-element.47), channel_id=1, source_target_pairs={{0,3},{1,0},{2,1},{3,2},{4,7},{5,4},{6,5},{7,6},{8,11},{9,8},{10,9... | collective-permute-start | bytes 98312 | tf_op jit(solution)/shard_map/ppermute | solution.py:37
  68.7 10.1 %collective-permute-start.27 = (bf16[256,256]{1,0:T(8,128)(2,1)S(1)}, bf16[256,256]{1,0:T(8,128)(2,1)S(1)}, u32[]{:S(2)}, u32[]{:S(2)}) collective-permute-start(bf16[256,256]{1,0:T(8,128)(2,1)S(1)} %collective-permute-done.16.a2), channel_id=1, source_target_pairs={{0,1},{1,0},{2,3},{3,2},{4,5},{5,4},{6,7},{7,6},{8,9},{9,8},{10,11... | collective-permute-start | bytes 393224 | tf_op jit(solution)/shard_map/ppermute | solution.py:37
  69.8 9.0 %collective-permute-start.28 = (bf16[256,256]{1,0:T(8,128)(2,1)S(1)}, bf16[256,256]{1,0:T(8,128)(2,1)S(1)}, u32[]{:S(2)}, u32[]{:S(2)}) collective-permute-start(bf16[256,256]{1,0:T(8,128)(2,1)S(1)} %collective-permute-done.18.a3), channel_id=1, source_target_pairs={{0,1},{1,0},{2,3},{3,2},{4,5},{5,4},{6,7},{7,6},{8,9},{9,8},{10,11... | collective-permute-start | bytes 393224 | tf_op jit(solution)/shard_map/ppermute | solution.py:37
  72.7 7.8 %collective-permute-start.23 = (bf16[64,768]{1,0:T(8,128)(2,1)S(1)}, bf16[64,768]{1,0:T(8,128)(2,1)S(1)}, u32[]{:S(2)}, u32[]{:S(2)}) collective-permute-start(bf16[64,768]{1,0:T(8,128)(2,1)S(1)} %cache_heads.1.after.c0), channel_id=1, source_target_pairs={{0,64},{1,65},{2,66},{3,67},{4,68},{5,69},{6,70},{7,71},{8,72},{9,... | collective-permute-start | bytes 294920 | tf_op jit(solution)/shard_map/ppermute | solution.py:37
  74.3 6.3 %collective-permute-start.24 = (bf16[64,768]{1,0:T(8,128)(2,1)S(1)}, bf16[64,768]{1,0:T(8,128)(2,1)S(1)}, u32[]{:S(2)}, u32[]{:S(2)}) collective-permute-start(bf16[64,768]{1,0:T(8,128)(2,1)S(1)} %cache_heads.1.after.c0), channel_id=1, source_target_pairs={{0,32},{1,33},{2,34},{3,35},{4,36},{5,37},{6,38},{7,39},{8,40},{9,... | collective-permute-start | bytes 294920 | tf_op jit(solution)/shard_map/ppermute | solution.py:37
  76.6 4.6 %collective-permute-start.25 = (bf16[64,768]{1,0:T(8,128)(2,1)S(1)}, bf16[64,768]{1,0:T(8,128)(2,1)S(1)}, u32[]{:S(2)}, u32[]{:S(2)}) collective-permute-start(bf16[64,768]{1,0:T(8,128)(2,1)S(1)} %cache_heads.1.after.c0), channel_id=1, source_target_pairs={{0,96},{1,97},{2,98},{3,99},{4,100},{5,101},{6,102},{7,103},{8,104... | collective-permute-start | bytes 294920 | tf_op jit(solution)/shard_map/ppermute | solution.py:37
  81.3 8.6 %collective-permute-start.29 = (bf16[4,64,768]{2,1,0:T(8,128)(2,1)S(1)}, bf16[4,64,768]{2,1,0:T(8,128)(2,1)S(1)}, u32[]{:S(2)}, u32[]{:S(2)}) collective-permute-start(bf16[4,64,768]{2,1,0:T(8,128)(2,1)S(1)} %cache_join.1.own), channel_id=1, source_target_pairs={{0,16},{1,17},{2,18},{3,19},{4,20},{5,21},{6,22},{7,23},{8,24},{9,... | collective-permute-start | bytes 1179656 | tf_op jit(solution)/shard_map/ppermute | solution.py:37
  81.4 6.0 %collective-permute-start.30 = (bf16[64,512]{1,0:T(8,128)(2,1)S(1)}, bf16[64,512]{1,0:T(8,128)(2,1)S(1)}, u32[]{:S(2)}, u32[]{:S(2)}) collective-permute-start(bf16[64,512]{1,0:T(8,128)(2,1)S(1)} %get-tuple-element.51), channel_id=1, source_target_pairs={{0,2},{1,3},{2,0},{3,1},{4,6},{5,7},{6,4},{7,5},{8,10},{9,11},{10,... | collective-permute-start | bytes 196616 | tf_op jit(solution)/shard_map/ppermute | solution.py:37
  82.6 4.8 %collective-permute-start.31 = (bf16[64,512]{1,0:T(8,128)(2,1)S(1)}, bf16[64,512]{1,0:T(8,128)(2,1)S(1)}, u32[]{:S(2)}, u32[]{:S(2)}) collective-permute-start(bf16[64,512]{1,0:T(8,128)(2,1)S(1)} %get-tuple-element.52), channel_id=1, source_target_pairs={{0,1},{1,2},{2,3},{3,0},{4,5},{5,6},{6,7},{7,4},{8,9},{9,10},{10,1... | collective-permute-start | bytes 196616 | tf_op jit(solution)/shard_map/ppermute | solution.py:37
  84.3 5.5 %collective-permute-start.32 = (bf16[64,512]{1,0:T(8,128)(2,1)S(1)}, bf16[64,512]{1,0:T(8,128)(2,1)S(1)}, u32[]{:S(2)}, u32[]{:S(2)}) collective-permute-start(bf16[64,512]{1,0:T(8,128)(2,1)S(1)} %get-tuple-element.53), channel_id=1, source_target_pairs={{0,3},{1,0},{2,1},{3,2},{4,7},{5,4},{6,5},{7,6},{8,11},{9,8},{10,9... | collective-permute-start | bytes 196616 | tf_op jit(solution)/shard_map/ppermute | solution.py:37
  (9 other events, 131.6 us)
